TPU v7x, 32 devices: a whole 2x2x4 slice. The times are simulated.
32 devices in a mesh: req: 8 (over z, y), head: 4 (over x, core).
Axes of the slice: x: 2, y: 2, z: 4, core: 2. Of those that a mesh axis runs over, the one named last changes fastest.
Arguments:
- hidden_in: bfloat16 [128, 2048], P('req'), may hold values from -6 to 6
- lengths: int32 [128], P('req'), may hold values from 1 to 4096, as said below
- page_request: int32 [512], P('req'), may hold values from 0 to 127, as said below
- page_fill: int32 [512], P('req'), may hold values from 0 to 128, as said below
- cache_keys: bfloat16 [512, 4, 128, 128], P('req', 'head'), may hold values from -400 to 400
- cache_values: bfloat16 [512, 4, 128, 128], P('req', 'head'), may hold values from -6 to 6
- attn_gain: float32 [2048], replicated, may hold values from 0.1 to 1.9
- query_weight: bfloat16 [2048, 2048], P(None, 'head'), may hold values from -0.125 to 0.125
- keyval_weight: bfloat16 [2048, 2, 512], P(None, None, 'head'), may hold values from -0.125 to 0.125
- out_weight: bfloat16 [2048, 2048], P('head'), may hold values from -0.125 to 0.125
- moe_gain: float32 [2048], replicated, may hold values from 0.1 to 1.9
- shared_gate_up: bfloat16 [2048, 2, 2816], P(None, None, 'head'), may hold values from -0.125 to 0.125
- shared_down: bfloat16 [2816, 2048], P('head'), may hold values from -0.109375 to 0.109375
- expert_gate_up: bfloat16 [16, 2048, 2, 1408], P('req', None, None, 'head'), may hold values from -0.125 to 0.125
- expert_down: bfloat16 [16, 1408, 2048], P('req', 'head'), may hold values from -0.15625 to 0.15625
- expert_ids: int32 [128, 6], P('req'), may hold values from 0 to 15, all different within a row; in each aligned block of 16 rows (0 to 15, 16 to 31, ...) at most 12 rows name the same one
- route_weights: float32 [128, 6], P('req'), may hold values from 0.1 to 0.6
Outputs:
- layer_out: bfloat16 [128, 2048], P('req', 'head')
Inputs may be any that keep to these rules, and one draw needn't show every extreme that they name: `lengths`: some request has exactly 4096 cached tokens. `page_request`: every request owns ceil(lengths / 128) pages, placed anywhere in the pool; the other pages are free. `page_fill`: live tokens fill a page's first slots: 128 in every page of a request but its last, the rest in the last, 0 in a free page. `expert_ids`: among the requests of one index of req no expert is named more than 12 times.
All inputs are finite; a program needn't handle non-finite values.
Results may differ from a plain program's by a relative error of at most 0.023.
Values may be sent and summed in bfloat16 or wider, within the bound.
No kernel may reach another device: no remote copies, remote signals or barrier semaphores. Data moves between devices by JAX's collectives and lax.ppermute only.
A program may use at most 128 MiB of HBM per device.

v0:
```python
import jax
import jax.numpy as jnp
from jax import lax
from jax.sharding import PartitionSpec as P

QPK = 4
HD = 128


EPSILON = 1e-06
ROPE_BASE = 600000.0
NEG_LARGE = -1e30


def rms_scale(values, gain_vector):
    return (
        values
        * lax.rsqrt(jnp.mean(values * values, axis=-1, keepdims=True) + EPSILON)
        * gain_vector
    )


def rotary(values, positions):
    half_dim = values.shape[-1] // 2
    frequency = ROPE_BASE ** (-2.0 * jnp.arange(half_dim, dtype=jnp.float32) / values.shape[-1])
    angles = positions.astype(jnp.float32)[:, None, None] * frequency[None, None, :]
    cosines = jnp.cos(angles)
    sine_part = jnp.sin(angles)
    first_half = values[..., :half_dim]
    second_half = values[..., half_dim:]
    return jnp.concatenate(
        [
            first_half * cosines - second_half * sine_part,
            second_half * cosines + first_half * sine_part,
        ],
        axis=-1,
    )


def local(
    hidden_in,
    lengths,
    page_request,
    page_fill,
    cache_keys,
    cache_values,
    attn_gain,
    query_weight,
    keyval_weight,
    out_weight,
    moe_gain,
    shared_gate_up,
    shared_down,
    expert_gate_up,
    expert_down,
    expert_ids,
    route_weights,
):
    rows_here = hidden_in.shape[0]
    model_width = hidden_in.shape[1]
    req_count = lax.axis_size("req")
    head_count = lax.axis_size("head")
    groups = keyval_weight.shape[2] // HD
    query_heads = groups * QPK
    all_rows = rows_here * req_count
    pages_here = page_request.shape[0]
    score_scale = HD ** (-0.5)
    inputs = hidden_in.astype(jnp.float32)
    normed = rms_scale(inputs, attn_gain).astype(jnp.bfloat16)
    query_local = rotary(
        jnp.dot(normed, query_weight, preferred_element_type=jnp.float32).reshape(
            rows_here, query_heads, HD
        ),
        lengths,
    ).astype(jnp.bfloat16)
    keyval = jnp.einsum("rd,dkc->rkc", normed, keyval_weight, preferred_element_type=jnp.float32)
    new_key = rotary(keyval[:, 0].reshape(rows_here, groups, HD), lengths).astype(jnp.bfloat16)
    new_value = keyval[:, 1].reshape(rows_here, groups, HD).astype(jnp.bfloat16)
    all_queries = lax.all_gather(
        query_local.reshape(rows_here, query_heads * HD), "req", axis=0, tiled=True
    )
    page_query = jnp.take(all_queries, page_request, axis=0).reshape(pages_here, groups, QPK, HD)
    scores = (
        jnp.einsum("pgjh,pgth->pgjt", page_query, cache_keys, preferred_element_type=jnp.float32)
        * score_scale
    )
    live_mask = (
        jnp.arange(cache_keys.shape[2], dtype=jnp.int32)[None, None, None, :]
        < page_fill[:, None, None, None]
    )
    masked = jnp.where(live_mask, scores, NEG_LARGE)
    page_max = jnp.max(masked, axis=-1)
    page_probs = jnp.where(live_mask, jnp.exp(masked - page_max[..., None]), 0.0).astype(
        jnp.bfloat16
    )
    page_sum = jnp.sum(page_probs.astype(jnp.float32), axis=-1).reshape(pages_here, query_heads)
    page_out = jnp.einsum(
        "pgjt,pgth->pgjh", page_probs, cache_values, preferred_element_type=jnp.float32
    ).reshape(pages_here, query_heads * HD)
    page_max = page_max.reshape(pages_here, query_heads)
    owner_hot = page_request[:, None] == jnp.arange(all_rows, dtype=jnp.int32)[None, :]
    cache_max = jnp.max(jnp.where(owner_hot[:, :, None], page_max[:, None, :], NEG_LARGE), axis=0)
    weight = jnp.exp(page_max - jnp.take(cache_max, page_request, axis=0))
    owner_matrix = owner_hot.astype(jnp.float32).T
    cache_sum = jnp.dot(owner_matrix, page_sum * weight, precision=lax.Precision.HIGHEST)
    cache_out = jnp.dot(
        owner_matrix, page_out * jnp.repeat(weight, HD, axis=1), precision=lax.Precision.HIGHEST
    )
    returned = (
        lax.all_to_all(
            cache_max.reshape(req_count, rows_here, query_heads),
            "req",
            split_axis=0,
            concat_axis=0,
            tiled=True,
        ),
        lax.all_to_all(
            cache_sum.reshape(req_count, rows_here, query_heads),
            "req",
            split_axis=0,
            concat_axis=0,
            tiled=True,
        ),
        lax.all_to_all(
            cache_out.reshape(req_count, rows_here, query_heads * HD),
            "req",
            split_axis=0,
            concat_axis=0,
            tiled=True,
        ),
    )
    own_max = jnp.max(returned[0], axis=0)
    source_scale = jnp.exp(returned[0] - own_max[None])
    own_sum = jnp.sum(returned[1] * source_scale, axis=0)
    own_out = jnp.sum(
        returned[2].reshape(req_count, rows_here, query_heads, HD) * source_scale[..., None], axis=0
    )
    key_rows = jnp.repeat(new_key, QPK, axis=1).astype(jnp.float32)
    value_rows = jnp.repeat(new_value, QPK, axis=1).astype(jnp.float32)
    new_score = jnp.sum(query_local.astype(jnp.float32) * key_rows, axis=-1) * score_scale
    total_max = jnp.maximum(own_max, new_score)
    old_scale = jnp.exp(own_max - total_max)
    new_scale = jnp.exp(new_score - total_max)
    denominator = own_sum * old_scale + new_scale
    numerator = own_out * old_scale[..., None] + new_scale[..., None] * value_rows
    attention = (
        (numerator / denominator[..., None])
        .reshape(rows_here, query_heads * HD)
        .astype(jnp.bfloat16)
    )
    attn_total = lax.psum(
        jnp.dot(attention, out_weight, preferred_element_type=jnp.float32).astype(jnp.bfloat16),
        "head",
    ).astype(jnp.float32)
    residual = inputs + attn_total
    moe_input = rms_scale(residual, moe_gain).astype(jnp.bfloat16)
    shared_pair = jnp.einsum(
        "rd,dkf->rkf", moe_input, shared_gate_up, preferred_element_type=jnp.float32
    )
    shared_act = (jax.nn.silu(shared_pair[:, 0]) * shared_pair[:, 1]).astype(jnp.bfloat16)
    shared_out = jnp.dot(shared_act, shared_down, preferred_element_type=jnp.float32)
    experts_here = expert_gate_up.shape[0]
    expert_total = experts_here * req_count
    top_count = expert_ids.shape[1]
    capacity = max(2, 2 * rows_here * top_count // expert_total)
    flat_ids = expert_ids.reshape(rows_here * top_count)
    expert_hot = (flat_ids[:, None] == jnp.arange(expert_total, dtype=jnp.int32)[None, :]).astype(
        jnp.int32
    )
    slot_ranks = jnp.sum((jnp.cumsum(expert_hot, axis=0) - expert_hot) * expert_hot, axis=1)
    slot_ids = flat_ids * capacity + slot_ranks
    slot_hot = (
        slot_ids[:, None] == jnp.arange(expert_total * capacity, dtype=jnp.int32)[None, :]
    ).astype(jnp.float32)
    token_hot = (
        (jnp.arange(rows_here * top_count, dtype=jnp.int32) // top_count)[:, None]
        == jnp.arange(rows_here, dtype=jnp.int32)[None, :]
    ).astype(jnp.float32)
    placement = jnp.dot(slot_hot.T, token_hot, precision=lax.Precision.HIGHEST).astype(jnp.bfloat16)
    blend = jnp.dot(
        token_hot.T,
        slot_hot * route_weights.reshape(rows_here * top_count)[:, None],
        precision=lax.Precision.HIGHEST,
    )
    quarter = model_width // head_count
    head_offset = lax.axis_index("head") * quarter
    outgoing = (
        jnp.dot(placement, moe_input, preferred_element_type=jnp.float32)
        .astype(jnp.bfloat16)
        .reshape(req_count, experts_here, capacity, moe_input.shape[1])
    )
    pair = jnp.einsum(
        "secd,edkf->seckf",
        lax.all_to_all(outgoing, "req", split_axis=0, concat_axis=0, tiled=True),
        expert_gate_up,
        preferred_element_type=jnp.float32,
    )
    expert_act = (jax.nn.silu(pair[:, :, :, 0]) * pair[:, :, :, 1]).astype(jnp.bfloat16)
    result = jnp.einsum(
        "secf,efd->secd", expert_act, expert_down, preferred_element_type=jnp.float32
    )
    arrived = lax.all_to_all(
        result.astype(jnp.bfloat16), "req", split_axis=0, concat_axis=0, tiled=True
    ).astype(result.dtype)
    routed = jnp.dot(
        blend,
        arrived.reshape(expert_total * capacity, arrived.shape[3]),
        precision=lax.Precision.HIGHEST,
    )
    residual_part = lax.dynamic_slice_in_dim(residual, head_offset, quarter, 1)
    head_term = shared_out + routed
    summed_head = lax.psum_scatter(
        head_term.astype(jnp.bfloat16), "head", scatter_dimension=1, tiled=True
    ).astype(jnp.float32)
    total = residual_part + summed_head
    return total.astype(jnp.bfloat16)


def solution(mesh):
    in_specs = (
        P("req", None),
        P("req"),
        P("req"),
        P("req"),
        P("req", "head", None, None),
        P("req", "head", None, None),
        P(),
        P(None, "head"),
        P(None, None, "head"),
        P("head", None),
        P(),
        P(None, None, "head"),
        P("head", None),
        P("req", None, None, "head"),
        P("req", "head", None),
        P("req", None),
        P("req", None),
    )
    out_specs = P("req", "head")
    return jax.shard_map(local, mesh=mesh, in_specs=in_specs, out_specs=out_specs, check_vma=False)
```

profile of v0, /device:TPU:0, one launch (start us, length us, event | category | flops | bytes accessed | tf_op | source)
XLA Modules:
  0.0 216.0 jit_solution(16841388622470495191)
XLA Ops:
  6.5 0.8 compare_select_fusion
  7.4 0.7 compare_and_fusion
  8.1 0.7 iota_compare_fusion.7
  8.8 1.0 fusion.34
  9.8 0.7 convert_element_type.94
  10.6 1.6 fusion.28
  12.3 2.1 fusion.70
  14.7 32.3 %all_gather.3 = bf16[128,512]{1,0:T(8,128)(2,1)S(1)} all-gather(bf16[16,512]{1,0:T(8,128)(2,1)S(1)} %bitcast.115), channel_id=1, replica_groups=mesh['req'=8,'head'=4] {'req'}, dimensions={0}, use_global_device_ids=true | all-gather | bytes 147456 | tf_op jit(solution)/shard_map/all_gather | solution.py:79
  47.1 0.7 gather_fusion
  47.9 2.9 %fusion.92 = (f32[64,4]{1,0:T(8,128)S(1)}, f32[64,4,128]{2,1,0:T(4,128)S(1)}) fusion(bf16[64,1,128,128]{3,2,1,0:T(8,128)(2,1)} %param.21, bf16[64,4,128]{2,1,0:T(4,128)(2,1)S(1)} %gather.11, pred[64]{0:T(512)(128)(4,1)S(1)} %compare_and_fusion, pred[64,128]{1,0:T(8,128)(4,1)S(1)} %iota_compare_fusion.8), kind=kOutput, calls=%fused_computation.132 | convolution fusion | flops 8519424 | bytes 2303040 | tf_op jit(solution)/shard_map/pgjh,pgth->pgjt/dot_general | solution.py:84
  51.1 0.6 copy.72
  51.7 5.5 %all-to-all-start.1 = ((f32[8,16,4]{1,2,0:T(4,128)}), f32[8,16,4]{1,2,0:T(4,128)S(1)}, u32[]{:S(2)}, u32[]{:S(2)}) async-start(f32[8,16,4]{1,2,0:T(4,128)} %copy.72), calls=%async_computation.1 | async-start | bytes 32768 | tf_op jit(solution)/shard_map/all_to_all | solution.py:110
  57.3 0.6 gather_fusion.1
  58.0 0.2 convert_reduce_fusion
  58.2 2.3 %fusion.24 = f32[64,4,128]{2,1,0:T(4,128)S(1)} fusion(bf16[64,1,128,128]{3,2,1,0:T(8,128)(2,1)} %param.22, f32[64,4]{1,0:T(8,128)S(1)} %subtract_exponential_fusion, f32[64,4,128]{2,1,0:T(4,128)S(1)} %get-tuple-element.21, f32[64,4]{1,0:T(8,128)S(1)} %get-tuple-element.20, pred[64,128]{1,0:T(8,128)(4,1)S(1)} %iota_compare_fusion.8), kind=kOutput, calls=%fused_computation.19 | convolution fusion | flops 8519680 | bytes 2369536 | tf_op jit(solution)/shard_map/pgjt,pgth->pgjh/dot_general | solution.py:97
  60.6 1.0 fusion.41
  61.6 1.0 fusion.39
  63.2 0.5 all-to-all-done.1
  63.8 5.5 %all-to-all-start.2 = ((f32[8,16,4]{1,2,0:T(4,128)}), f32[8,16,4]{1,2,0:T(4,128)S(1)}, u32[]{:S(2)}, u32[]{:S(2)}) async-start(f32[8,16,4]{1,2,0:T(4,128)} %fusion.39), calls=%async_computation.2 | async-start | bytes 32768 | tf_op jit(solution)/shard_map/all_to_all | solution.py:117
  69.2 0.6 and_select_fusion
  69.9 5.9 %all-to-all-done.2 = f32[8,16,4]{1,2,0:T(4,128)S(1)} async-done(((f32[8,16,4]{1,2,0:T(4,128)}), f32[8,16,4]{1,2,0:T(4,128)S(1)}, u32[]{:S(2)}, u32[]{:S(2)}) %all-to-all-start.2) | async-done | bytes 2080 | tf_op jit(solution)/shard_map/all_to_all | solution.py:117
  75.9 3.4 %all-to-all-start = ((f32[8,16,512]{2,1,0:T(8,128)}), f32[8,16,512]{2,1,0:T(8,128)S(1)}, u32[]{:S(2)}, u32[]{:S(2)}) async-start(f32[8,16,512]{2,1,0:T(8,128)} %fusion.41), calls=%async_computation | async-start | bytes 524288 | tf_op jit(solution)/shard_map/all_to_all | solution.py:124
  79.3 0.6 multiply_reduce_fusion.3
  80.3 0.8 mul.267
  81.1 0.7 multiply_add_fusion.2
  82.1 5.3 %all-to-all-done = f32[8,16,512]{2,1,0:T(8,128)S(1)} async-done(((f32[8,16,512]{2,1,0:T(8,128)}), f32[8,16,512]{2,1,0:T(8,128)S(1)}, u32[]{:S(2)}, u32[]{:S(2)}) %all-to-all-start) | async-done | bytes 262176 | tf_op jit(solution)/shard_map/all_to_all | solution.py:124
  87.5 1.0 multiply_reduce_fusion
  88.6 2.6 %convolution_convert_fusion.1 = bf16[16,2048]{1,0:T(8,128)(2,1)} fusion(bf16[512,2048]{1,0:T(8,128)(2,1)} %param.26, f32[2,8,4,128]{3,2,1,0:T(4,128)S(1)} %bitcast.113, f32[2,8,4,128]{3,2,1,0:T(4,128)S(1)} %bitcast.114, f32[16,512]{1,0:T(8,128)S(1)} %multiply_reduce_fusion, f32[2,8,4,128]{3,2,1,0:T(4,128)S(1)} %bitcast.112), kind=kOutput, calls=%fused_computation.11 | convolution fusion | flops 33619968 | bytes 2293760 | tf_op jit(solution)/shard_map/dot_general | solution.py:152
  91.2 0.9 convolution_convert_fusion.2
  92.2 28.6 %all-reduce.2.cloned.1.call-done = bf16[16,2048]{1,0:T(8,128)(2,1)} async-done(((bf16[16,2048]{1,0:T(8,128)(2,1)}), bf16[16,2048]{1,0:T(8,128)(2,1)}) %all-reduce.2.cloned.1.call-update) | async-done | bytes 65552 | tf_op jit(solution)/shard_map/psum | solution.py:151
  120.7 1.0 convert_add_fusion
  121.7 2.2 %convolution_convert_fusion = bf16[192,2048]{1,0:T(8,128)(2,1)} fusion(bf16[192,16]{0,1:T(8,128)(2,1)S(1)} %convolution_convert_fusion.2, f32[2048]{0:T(1024)S(1)} %copy-done.4, f32[16]{0:T(128)S(1)} %add_rsqrt_fusion, bf16[16,2048]{1,0:T(8,128)(2,1)} %all-reduce.2.cloned.1.call-done, bf16[16,2048]{1,0:T(8,128)(2,1)S(1)} %copy-done.2), kind=kOutput, calls=%fused_computation.7 | convolution fusion | flops 13172736 | bytes 931904 | tf_op jit(solution)/shard_map/dot_general | solution.py:188
  123.9 2.1 reshape.375
  126.0 2.0 copy.82
  128.1 24.5 %all_to_all.25 = bf16[8,2,12,2048]{3,1,2,0:T(2,128)(2,1)S(1)} all-to-all(bf16[8,2,12,2048]{3,1,2,0:T(2,128)(2,1)S(1)} %copy.82), channel_id=1, replica_groups=mesh['req'=8,'head'=4] {'req'}, dimensions={0} | all-to-all | bytes 1572864 | tf_op jit(solution)/shard_map/all_to_all | solution.py:194
  152.5 4.7 %fusion.15 = f32[8,2,12,2,352]{4,2,3,0,1:T(8,128)S(1)} fusion(bf16[2,2048,2,352]{1,3,2,0:T(8,128)(2,1)} %param.30, bf16[8,2,12,2048,1]{3,1,2,0,4:T(2,128)(2,1)S(1)} %bitcast.111), kind=kOutput, calls=%fused_computation.16 | convolution fusion | flops 553648128 | bytes 7094272 | tf_op jit(solution)/shard_map/secd,edkf->seckf/dot_general | solution.py:192
  157.2 0.7 fusion.7
  158.0 1.7 copy.85
  159.7 4.2 %all-to-all-start.4 = ((bf16[8,2,12,2048]{3,1,2,0:T(2,128)(2,1)}), bf16[8,2,12,2048]{3,1,2,0:T(2,128)(2,1)}, u32[]{:S(2)}, u32[]{:S(2)}) async-start(bf16[8,2,12,2048]{3,1,2,0:T(2,128)(2,1)} %copy.85), calls=%async_computation.4 | async-start | bytes 1572864 | tf_op jit(solution)/shard_map/all_to_all | solution.py:202
  164.4 0.3 fusion.37
  164.7 4.4 %fusion.43 = f32[16,2,704]{2,0,1:T(8,128)S(1)} fusion(bf16[2048,2,704]{0,2,1:T(8,128)(2,1)} %param.28, f32[2048]{0:T(1024)S(1)} %copy-done.4, f32[16]{0:T(128)S(1)} %add_rsqrt_fusion, bf16[16,2048]{1,0:T(8,128)(2,1)S(1)} %copy-done.3, bf16[16,2048]{1,0:T(8,128)(2,1)S(1)} %copy-done.2), kind=kOutput, calls=%fused_computation.48 | convolution fusion | flops 92471296 | bytes 5996608 | tf_op jit(solution)/shard_map/rd,dkf->rkf/dot_general | solution.py:157
  169.1 0.5 fusion.63
  169.6 13.6 %all-to-all-done.4 = bf16[8,2,12,2048]{3,1,2,0:T(2,128)(2,1)} async-done(((bf16[8,2,12,2048]{3,1,2,0:T(2,128)(2,1)}), bf16[8,2,12,2048]{3,1,2,0:T(2,128)(2,1)}, u32[]{:S(2)}, u32[]{:S(2)}) %all-to-all-start.4) | async-done | bytes 786464 | tf_op jit(solution)/shard_map/all_to_all | solution.py:202
  183.2 2.4 %copy.86 = bf16[8,2,12,2048]{3,2,1,0:T(8,128)(2,1)} copy(bf16[8,2,12,2048]{3,1,2,0:T(2,128)(2,1)} %all-to-all-done.4) | data formatting | bytes 1572864 | tf_op jit(solution)/shard_map/all_to_all | solution.py:202
  185.6 2.1 reshape.376
  187.7 2.2 %fusion.10 = bf16[16,2048]{1,0:T(8,128)(2,1)} fusion(f32[16,2048]{1,0:T(8,128)S(1)} %fusion.63, f32[16,192]{1,0:T(8,128)S(1)} %fusion.37, bf16[192,2048]{1,0:T(8,128)(2,1)} %reshape.376), kind=kOutput, calls=%fused_computation.10 | convolution fusion | flops 75563008 | bytes 995328 | tf_op jit(solution)/shard_map/dot_general | solution.py:205
  189.9 17.9 %reduce-scatter.2.cloned.1.call-done = bf16[16,512]{1,0:T(8,128)(2,1)} async-done(((bf16[16,2048]{1,0:T(8,128)(2,1)}), bf16[16,512]{1,0:T(8,128)(2,1)}) %reduce-scatter.2.cloned.1.call-update) | async-done | bytes 16400 | tf_op jit(solution)/shard_map/reduce_scatter | solution.py:212
  207.9 1.3 add_convert_fusion
  (64 shorter events, 3.3 us)
Async XLA Ops:
  6.5 150.7 %copy-start = (bf16[2,352,2048]{2,1,0:T(8,128)(2,1)S(1)}, bf16[2,352,2048]{2,1,0:T(8,128)(2,1)}, u32[]{:S(2)}) copy-start(bf16[2,352,2048]{2,1,0:T(8,128)(2,1)} %param.31) | copy-start | bytes 8650756
  10.6 37.2 %copy-start.8 = (s32[64]{0:T(128)S(1)}, s32[64]{0:T(128)}, u32[]{:S(2)}) copy-start(s32[64]{0:T(128)} %param.20) | copy-start | bytes 772
  50.8 9.8 %copy-start.5 = (s32[64]{0:T(128)S(1)}, s32[64]{0:T(128)}, u32[]{:S(2)}) copy-start(s32[64]{0:T(128)} %param.19) | copy-start | bytes 772
  50.8 11.9 %copy-start.6 = (s32[16,6]{0,1:T(8,128)S(1)}, s32[16,6]{0,1:T(8,128)}, u32[]{:S(2)}) copy-start(s32[16,6]{0,1:T(8,128)} %param.32) | copy-start | bytes 1156
  51.7 12.1 %all-to-all-start.1 = ((f32[8,16,4]{1,2,0:T(4,128)}), f32[8,16,4]{1,2,0:T(4,128)S(1)}, u32[]{:S(2)}, u32[]{:S(2)}) async-start(f32[8,16,4]{1,2,0:T(4,128)} %copy.72), calls=%async_computation.1 | async-start | bytes 32768 | tf_op jit(solution)/shard_map/all_to_all | solution.py:110
  63.8 12.1 %all-to-all-start.2 = ((f32[8,16,4]{1,2,0:T(4,128)}), f32[8,16,4]{1,2,0:T(4,128)S(1)}, u32[]{:S(2)}, u32[]{:S(2)}) async-start(f32[8,16,4]{1,2,0:T(4,128)} %fusion.39), calls=%async_computation.2 | async-start | bytes 32768 | tf_op jit(solution)/shard_map/all_to_all | solution.py:117
  75.9 11.6 %all-to-all-start = ((f32[8,16,512]{2,1,0:T(8,128)}), f32[8,16,512]{2,1,0:T(8,128)S(1)}, u32[]{:S(2)}, u32[]{:S(2)}) async-start(f32[8,16,512]{2,1,0:T(8,128)} %fusion.41), calls=%async_computation | async-start | bytes 524288 | tf_op jit(solution)/shard_map/all_to_all | solution.py:124
  79.3 41.4 %all-reduce.2.cloned.1.call-start = ((), (), s32[]{:S(2)}) async-start(), calls=%async_computation.6 | async-start | bytes 131072 | tf_op jit(solution)/shard_map/psum | solution.py:151
  79.9 40.8 %copy-start.2 = (bf16[16,2048]{1,0:T(8,128)(2,1)S(1)}, bf16[16,2048]{1,0:T(8,128)(2,1)}, u32[]{:S(2)}) copy-start(bf16[16,2048]{1,0:T(8,128)(2,1)} %param.17) | copy-start | bytes 196612
  80.3 41.4 %copy-start.4 = (f32[2048]{0:T(1024)S(1)}, f32[2048]{0:T(1024)}, u32[]{:S(2)}) copy-start(f32[2048]{0:T(1024)} %param.27) | copy-start | bytes 24580
  158.0 6.2 %copy-start.7 = (f32[16,6]{0,1:T(8,128)S(1)}, f32[16,6]{0,1:T(8,128)}, u32[]{:S(2)}) copy-start(f32[16,6]{0,1:T(8,128)} %param.33) | copy-start | bytes 1156
  158.0 6.4 %copy-start.9 = (s32[96]{0:T(128)S(1)}, s32[96]{0:T(128)}, u32[]{:S(2)}) copy-start(s32[96]{0:T(128)} %get-tuple-element.22) | copy-start | bytes 1156
  158.0 6.4 %copy-start.10 = (s32[96]{0:T(128)S(1)}, s32[96]{0:T(128)}, u32[]{:S(2)}) copy-start(s32[96]{0:T(128)} %get-tuple-element.23) | copy-start | bytes 1156
  158.0 6.6 %copy-start.3 = (bf16[16,2048]{1,0:T(8,128)(2,1)S(1)}, bf16[16,2048]{1,0:T(8,128)(2,1)}, u32[]{:S(2)}) copy-start(bf16[16,2048]{1,0:T(8,128)(2,1)} %all-reduce.2.cloned.1.call-done) | copy-start | bytes 196612
  159.7 23.4 %all-to-all-start.4 = ((bf16[8,2,12,2048]{3,1,2,0:T(2,128)(2,1)}), bf16[8,2,12,2048]{3,1,2,0:T(2,128)(2,1)}, u32[]{:S(2)}, u32[]{:S(2)}) async-start(bf16[8,2,12,2048]{3,1,2,0:T(2,128)(2,1)} %copy.85), calls=%async_computation.4 | async-start | bytes 1572864 | tf_op jit(solution)/shard_map/all_to_all | solution.py:202
  163.9 43.9 %reduce-scatter.2.cloned.1.call-start = ((), (), s32[]{:S(2)}) async-start(), calls=%async_computation.7 | async-start | bytes 81920 | tf_op jit(solution)/shard_map/reduce_scatter | solution.py:212
  164.7 4.4 %copy-start.1 = (bf16[704,2048]{1,0:T(8,128)(2,1)S(1)}, bf16[704,2048]{1,0:T(8,128)(2,1)}, u32[]{:S(2)}) copy-start(bf16[704,2048]{1,0:T(8,128)(2,1)} %param.29) | copy-start | bytes 8650756
Sparse Core Ops, SparseCore 0:
  91.4 29.3 all-reduce.1
  190.1 17.7 reduce-scatter.1
where the time goes:
time: 217 us; the launch traced here: 216 us
  waiting for transfers between devices  72 us (33%)
  blocking collectives  56.8 us (26%)
  matrix products  29.3 us (14%)
  starting transfers between devices  18.9 us (9%)
  local copies, waits for them, and re-layouts  14.7 us (7%)
  between operations  13.7 us (6%)
  other arithmetic  10.7 us (5%)
    all_gather x1, blocking collectives, local(): lax.all_gather(query_local.reshape(rows_here, query_heads * HD), 'req', a...  32.3 us
    psum x1, waiting for transfers between devices, local(): lax.psum(jnp.dot(attention, out_weight, preferred_element_type=jnp.float3...  28.6 us
    all_to_all x1, blocking collectives, local(): lax.all_to_all(outgoing, 'req', split_axis=0, concat_axis=0, tiled=True)  24.5 us
    reduce_scatter x1, waiting for transfers between devices, local(): lax.psum_scatter(head_term.astype(jnp.bfloat16), 'head', scatter_dimensio...  17.9 us
    all_to_all x1, waiting for transfers between devices, local(): lax.all_to_all(result.astype(jnp.bfloat16), 'req', split_axis=0, concat_a...  13.6 us
    all_to_all x1, waiting for transfers between devices, local(): lax.all_to_all(cache_sum.reshape(req_count, rows_here, query_heads), 'req...  5.95 us
    all_to_all x1, starting transfers between devices, local(): lax.all_to_all(cache_max.reshape(req_count, rows_here, query_heads), 'req...  5.51 us
    all_to_all x1, starting transfers between devices, local(): lax.all_to_all(cache_sum.reshape(req_count, rows_here, query_heads), 'req...  5.48 us
  transfers between devices with their start and end apart: 6, of which 6 were waited for; matrix products, arithmetic and copies ran while one was open for 7% of the time, Pallas kernels for 0%

commit v1 on v0

v1 whole, which is shorter than its diff:
```python
import functools
import math

import jax
import jax.numpy as jnp
import numpy as np
from jax import lax
from jax.experimental import pallas as pl
from jax.experimental.pallas import tpu as pltpu
from jax.sharding import Mesh
from jax.sharding import PartitionSpec as P

QPK = 4
HD = 128

EPSILON = 1e-06
ROPE_BASE = 600000.0
NEG_LARGE = -1e30
BF = jnp.bfloat16
F32 = jnp.float32
I32 = jnp.int32
VMEM = pl.BlockSpec(memory_space=pltpu.VMEM)
HBM = pl.BlockSpec(memory_space=pltpu.HBM)
REQ = ("ru", "rl")
HEAD = ("hu", "hl")
NT = (((1,), (1,)), ((), ()))
TN = (((0,), (0,)), ((), ()))


def rms_scale(values, gain_vector):
    return (
        values
        * lax.rsqrt(jnp.mean(values * values, axis=-1, keepdims=True) + EPSILON)
        * gain_vector
    )


def index_of(axes):
    return lax.axis_index(axes[0]) * lax.axis_size(axes[1]) + lax.axis_index(axes[1])


def size_of(axes):
    return lax.axis_size(axes[0]) * lax.axis_size(axes[1])


def swap(value, req_step, head_step=0):
    heads = size_of(HEAD)
    count = size_of(REQ) * heads
    step = req_step * heads + head_step
    return lax.ppermute(value, REQ + HEAD, [(i, i ^ step) for i in range(count)])


def stages(count, first):
    found, shift = [], 0
    while count > 1:
        size = min(count, 4 if shift else first)
        found.append((shift, size))
        shift += size.bit_length() - 1
        count //= size
    return found


def trade(whole, half, shift):
    heads = size_of(HEAD)
    count = size_of(REQ) * heads
    steps = [(2 << shift) * heads, (3 << shift) * heads]
    came = lax.ppermute(whole, REQ + HEAD, [(i, i ^ steps[i % 2]) for i in range(count)])
    return jnp.concatenate([half, came, swap(half, 1 << shift)], axis=0)


def position(index, plan):
    place, scale = 0, 1
    for shift, size in reversed(plan):
        place = place + ((index >> shift) & (size - 1)) * scale
        scale *= size
    return place


def gather(block, plan):
    for shift, size in reversed(plan):
        block = jnp.concatenate(
            [block] + [swap(block, i << shift) for i in range(1, size)], axis=0
        )
    return block


def joined(*arrays):
    return lax.optimization_barrier(arrays)


def deliver(blocks, plan):
    for shift, size in plan:
        part = blocks.shape[1] // size
        blocks = jnp.concatenate(
            [blocks[:, :part]]
            + [swap(blocks[:, i * part : (i + 1) * part], i << shift) for i in range(1, size)],
            axis=0,
        )
    return blocks


def scatter(blocks, plan):
    for shift, size in plan:
        part = blocks.shape[0] // size
        total = blocks[:part]
        for i in (size - 1, *range(1, size - 1)):
            sent = blocks[i * part : (i + 1) * part].astype(BF)
            total = total + swap(sent, i << shift).astype(F32)
        blocks = total
    return blocks


def call(kernel, out_shape, args, specs=None, scratch=(), mib=24, flops=0, nbytes=0):
    return pl.pallas_call(
        kernel,
        out_shape=out_shape,
        in_specs=specs or [VMEM] * len(args),
        out_specs=jax.tree.map(lambda _: VMEM, out_shape),
        scratch_shapes=list(scratch),
        compiler_params=pltpu.CompilerParams(vmem_limit_bytes=mib << 20),
        cost_estimate=pl.CostEstimate(flops=flops, bytes_accessed=nbytes, transcendentals=0),
    )(*args)


def in_hbm(*arrays):
    return tuple(pltpu.with_memory_space_constraint(a, pltpu.HBM) for a in arrays)


def stage(parts, *refs):
    count = len(parts)
    sources = [r if p is None else r.at[p] for r, p in zip(refs[1 : 1 + count], parts)]
    copies = fetch(list(zip(sources, refs[1 + count : -1])), refs[-1])
    for copy in copies:
        copy.wait()


def staged(after, *pairs):
    arrays, parts = zip(*[p if isinstance(p, tuple) else (p, None) for p in pairs])
    shapes = [a.shape if p is None else a.shape[1:] for a, p in zip(arrays, parts)]
    return call(
        functools.partial(stage, parts),
        tuple(pltpu.VMEM(shape, a.dtype) for shape, a in zip(shapes, arrays)),
        (after,) + in_hbm(*arrays),
        specs=[HBM] * (1 + len(arrays)),
        scratch=(pltpu.SemaphoreType.DMA((len(arrays),)),),
        mib=1,
        nbytes=sum(2 * math.prod(shape) for shape in shapes),
    )


def fetch(pairs, sem):
    copies = [pltpu.make_async_copy(a, b, sem.at[i]) for i, (a, b) in enumerate(pairs)]
    for copy in copies:
        copy.start()
    return copies


def cos_sin(angle):
    turns = jnp.floor(angle * (2.0 / 3.141592653589793) + 0.5)
    rest = angle - turns * 1.5703125
    rest = rest - turns * 4.837512969970703125e-4
    rest = rest - turns * 7.54978995489188216e-8
    square = rest * rest
    sine = ((-1.9515295891e-4 * square + 8.3321608736e-3) * square - 1.6666654611e-1) * square
    sine = sine * rest + rest
    cosine = (2.443315711809948e-5 * square - 1.388731625493765e-3) * square + 4.166664568298827e-2
    cosine = cosine * square * square - 0.5 * square + 1.0
    turns = turns.astype(I32)
    odd = (turns & 1) == 1
    cosine, sine = jnp.where(odd, sine, cosine), jnp.where(odd, cosine, sine)
    cosine = jnp.where(((turns + 1) & 2) == 2, -cosine, cosine)
    sine = jnp.where((turns & 2) == 2, -sine, sine)
    return cosine, sine


def project(
    lengths_hbm, freq_hbm, ids_hbm, route_hbm, hidden_hbm, gain_hbm, weight_hbm, out_ref, turn_ref, norm_ref,
    lengths, freq, ids, routes, hidden, gain, weight, sem,
):
    chunks = sem.shape[0] - 6
    deep = weight.shape[0] // chunks
    parts = [pl.ds(i * deep, deep) for i in range(chunks)]
    *heavy, early, late, first, second, third, last = fetch(
        [(weight_hbm.at[p], weight.at[p]) for p in parts]
        + [
            (lengths_hbm, lengths),
            (freq_hbm, freq),
            (ids_hbm, ids),
            (route_hbm, routes),
            (hidden_hbm, hidden),
            (gain_hbm, gain),
        ],
        sem,
    )
    copies = [early, late, first, second, third, last, *heavy]
    width = weight.shape[1]
    rows = hidden.shape[0]
    copies[0].wait()
    copies[1].wait()
    diagonal = lax.broadcasted_iota(I32, (rows, rows), 0) == lax.broadcasted_iota(
        I32, (rows, rows), 1
    )
    positions = jnp.sum(
        jnp.where(diagonal, lengths[...].astype(F32), 0.0), axis=1, keepdims=True
    )
    cosine, sine = cos_sin(positions * freq[...])
    sine = jnp.where(lax.broadcasted_iota(I32, sine.shape, 1) < HD // 2, -sine, sine)
    turn_ref[:, :HD] = cosine
    turn_ref[:, HD : 2 * HD] = sine
    core = lax.axis_index(HEAD[1]).astype(F32)
    turn_ref[:, 2 * HD :] = jnp.broadcast_to(core, (rows, HD))
    copies[2].wait()
    copies[3].wait()
    route = routes[...]
    heavy = route.astype(BF).astype(F32)
    lines = jnp.concatenate([ids[...].astype(F32), heavy, route - heavy], axis=0).astype(BF)
    shape = (lines.shape[0], HD)
    eye = lax.broadcasted_iota(I32, shape, 0) == lax.broadcasted_iota(I32, shape, 1)
    out_ref[:, width:] = lax.dot_general(
        lines, jnp.where(eye, 1.0, 0.0).astype(BF), TN, preferred_element_type=F32
    ).astype(BF)
    copies[4].wait()
    copies[5].wait()
    normed = rms_scale(hidden[...].astype(F32), gain[...]).astype(BF)
    norm_ref[...] = normed
    query = jnp.zeros((rows, width), F32)
    for i in range(chunks):
        copies[6 + i].wait()
        part = slice(i * deep, (i + 1) * deep)
        query = query + jnp.dot(normed[:, part], weight[part], preferred_element_type=F32)
    for i in range(width // HD):
        part = query[:, i * HD : (i + 1) * HD]
        turned = part * cosine + pltpu.roll(part, HD // 2, 1) * sine
        out_ref[:, i * HD : (i + 1) * HD] = turned.astype(BF)


def attend(
    query_ref, column_ref, row_ref, fill_ref, keys, values, out_ref,
    scores, probs, out_buf,
):
    pages = keys.shape[0]
    rows = query_ref.shape[0]
    lines = pages * QPK
    slots = keys.shape[1]
    hot = lax.broadcasted_iota(I32, (lines, QPK * rows), 1) == column_ref[...]
    stacked = jnp.concatenate([query_ref[:, i * HD : (i + 1) * HD] for i in range(QPK)], axis=0)
    query = jnp.dot(
        jnp.where(hot, 1.0, 0.0).astype(BF), stacked, preferred_element_type=F32
    ).astype(BF)
    some = 4
    span = some * slots
    for g in range(pages // some):
        part = slice(g * some * QPK, (g + 1) * some * QPK)
        key = keys[g * some : (g + 1) * some].reshape(span, HD)
        scores[part] = lax.dot_general(query[part], key, NT, preferred_element_type=F32)
    slot = lax.broadcasted_iota(I32, (lines, span), 1)
    first = (lax.broadcasted_iota(I32, (lines, 1), 0) // QPK) % some * slots
    live = (slot >= first) & (slot < first + fill_ref[...])
    score = jnp.where(live, scores[...] * (HD ** (-0.5)), NEG_LARGE)
    page_max = jnp.max(score, axis=1, keepdims=True)
    prob = jnp.where(live, jnp.exp(score - page_max), 0.0).astype(BF)
    probs[...] = prob
    page_sum = jnp.sum(prob.astype(F32), axis=1, keepdims=True)
    for g in range(pages // some):
        part = slice(g * some * QPK, (g + 1) * some * QPK)
        value = values[g * some : (g + 1) * some].reshape(span, HD)
        out_buf[part] = jnp.dot(probs[part], value, preferred_element_type=F32)
    held_max = jnp.max(jnp.where(hot, page_max, NEG_LARGE), axis=0, keepdims=True)
    back = jnp.sum(jnp.where(hot, held_max, 0.0), axis=1, keepdims=True)
    weight = jnp.exp(page_max - back)
    held_sum = jnp.sum(jnp.where(hot, page_sum * weight, 0.0), axis=0, keepdims=True)
    turned = lax.broadcasted_iota(I32, (QPK * rows, lines), 0) == row_ref[...]
    held_out = jnp.dot(
        jnp.where(turned, 1.0, 0.0).astype(BF),
        (out_buf[...] * weight).astype(BF),
        preferred_element_type=F32,
    )
    for i in range(QPK):
        out_ref[:, i * HD : (i + 1) * HD] = held_out[i * rows : (i + 1) * rows].astype(BF)
    rest = jnp.concatenate(
        [held_max[:, i * rows : (i + 1) * rows] for i in range(QPK)]
        + [held_sum[:, i * rows : (i + 1) * rows] for i in range(QPK)],
        axis=0,
    )
    terms = []
    for _ in range(3):
        term = rest.astype(BF).astype(F32)
        terms.append(term)
        rest = rest - term
    terms.append(jnp.zeros((HD - 6 * QPK, rows), F32))
    out_ref[:, QPK * HD :] = jnp.concatenate(terms, axis=0).T.astype(BF)


def combine(
    came_ref, query_ref, kv_ref, weight_ref, keep_ref, send_ref
):
    sources, rows = came_ref.shape[0], came_ref.shape[1]
    stats = came_ref[:, :, QPK * HD :].astype(F32).reshape(sources * rows, HD)
    step = 2 * QPK
    stats = stats[:, :step] + stats[:, step : 2 * step] + stats[:, 2 * step : 3 * step]
    stats = stats.reshape(sources, rows, step)
    part_max, part_sum = stats[:, :, :QPK], stats[:, :, QPK:]
    own_max = jnp.max(part_max, axis=0)
    key = kv_ref[:, :HD].astype(F32)
    value = kv_ref[:, HD:].astype(F32)
    new_score = jnp.concatenate(
        [
            jnp.sum(query_ref[:, i * HD : (i + 1) * HD].astype(F32) * key, axis=1, keepdims=True)
            for i in range(QPK)
        ],
        axis=1,
    ) * (HD ** (-0.5))
    top = jnp.maximum(own_max, new_score)
    new_scale = jnp.exp(new_score - top)
    scale = jnp.exp(part_max - top[None])
    denominator = jnp.sum(scale * part_sum, axis=0) + new_scale
    attention = []
    for i in range(QPK):
        total = new_scale[:, i : i + 1] * value
        for s in range(sources):
            total = total + scale[s, :, i : i + 1] * came_ref[
                s, :, i * HD : (i + 1) * HD
            ].astype(F32)
        attention.append((total / denominator[:, i : i + 1]).astype(BF))
    wide = jnp.dot(
        jnp.concatenate(attention, axis=1), weight_ref[...], preferred_element_type=F32
    )
    keep_ref[...] = wide
    send_ref[...] = wide.astype(BF)


def shared_kernel(
    residual_ref, gain_ref, gate_ref, down_ref, up_hbm, out_ref, up_ref, sem
):
    copies = fetch(((up_hbm.at[1], up_ref),), sem)
    inputs = rms_scale(residual_ref[...], gain_ref[...]).astype(BF)
    gate = lax.dot_general(inputs, gate_ref[...], NT, preferred_element_type=F32)
    copies[0].wait()
    up = lax.dot_general(inputs, up_ref[...], NT, preferred_element_type=F32)
    act = (jax.nn.silu(gate) * up).astype(BF)
    out_ref[...] = jnp.dot(act, down_ref[...], preferred_element_type=F32)


def blocks_of(step):
    head = index_of(HEAD)
    return lambda i, size: pl.ds(pl.multiple_of((head ^ (2 * i + step)) * size, HD), size)


def down_product(acts, down, shared_ref, out_ref, step):
    few = shared_ref.shape[0]
    size = out_ref.shape[2]
    place = blocks_of(step)
    for i in range(out_ref.shape[0]):
        at = place(i, size)
        out = sum(
            jnp.dot(act[...], down[e, :, at], preferred_element_type=F32)
            for e, act in enumerate(acts)
        )
        out_ref[i, :few] = (out[:few] + shared_ref[:, at]).astype(out_ref.dtype)
        out_ref[i, few:] = out[few:].astype(out_ref.dtype)


def keep_kernel(acts_ref, down_ref, shared_ref, keep_ref):
    acts = [acts_ref.at[e] for e in range(acts_ref.shape[0])]
    down_product(acts, down_ref, shared_ref, keep_ref, 0)


def experts_kernel(routes, count, *refs):
    here, there, here_other, there_other, gain_ref, routing_ref, shared_ref = refs[:7]
    expert_up = refs[7 : 7 + count]
    down_hbm, send_ref, acts_ref, down_ref, inputs, squares, sem = refs[7 + count :]
    copies = fetch([(down_hbm.at[e], down_ref.at[e]) for e in range(count)], sem)
    lines, size = here.shape
    core = lax.axis_index(HEAD[1])
    few = shared_ref.shape[0]
    squares[...] = jnp.zeros(squares.shape, F32)

    def put(rows, columns, values):
        values = values.astype(F32)
        squares[rows] += jnp.sum(values * values, axis=1, keepdims=True)
        inputs[rows, columns] = (values * gain_ref[:, columns]).astype(BF)

    for y, pair in enumerate(((here, here_other), (there, there_other))):
        for c, ref in zip((core, 1 - core), pair):
            half = pl.ds(pl.multiple_of(c * size, HD), size)
            for k in range(0, lines, 4 * few):
                row = y * lines + k
                third = pl.ds(pl.multiple_of(row + (2 + c) * few, 16), few)
                put(pl.ds(row, few), half, ref[k : k + few])
                put(third, pl.ds(0, size), ref[k + few : k + 2 * few])
                put(third, pl.ds(size, size), ref[k + 2 * few : k + 3 * few])
                put(pl.ds(row + few, few), half, ref[k + 3 * few : k + 4 * few])
    scale = lax.rsqrt(squares[:, :1] / (2 * size) + EPSILON)
    routing = routing_ref[...].astype(F32)
    ids = routing[:, :routes]
    weights = routing[:, routes : 2 * routes] + routing[:, 2 * routes : 3 * routes]
    for e in range(count):
        index = (index_of(REQ) * count + e).astype(F32)
        factor = jnp.sum(jnp.where(ids == index, weights, 0.0), axis=1, keepdims=True)
        gate = lax.dot_general(inputs[...], expert_up[e][0], NT, preferred_element_type=F32)
        up = lax.dot_general(inputs[...], expert_up[e][1], NT, preferred_element_type=F32)
        act = jax.nn.silu(gate * scale) * (up * scale) * factor
        acts_ref[e] = act.astype(BF)
    for copy in copies:
        copy.wait()
    acts = [acts_ref.at[e] for e in range(count)]
    down_product(acts, down_ref, shared_ref, send_ref, 1)


def local(
    hidden_in,
    lengths,
    page_request,
    page_fill,
    cache_keys,
    cache_values,
    attn_gain,
    query_weight,
    keyval_weight,
    out_weight,
    moe_gain,
    shared_gate_up,
    shared_down,
    expert_gate_up,
    expert_down,
    expert_ids,
    route_weights,
):
    rows, width = hidden_in.shape
    req_count = size_of(REQ)
    head_count = size_of(HEAD)
    req = index_of(REQ)
    wide = QPK * HD
    all_rows = rows * req_count
    pages = page_request.shape[0]
    top = expert_ids.shape[1]
    quarter = width // head_count
    plan = stages(req_count, 2)
    far = head_count // 2

    half = HD // 2
    frequency = np.tile(ROPE_BASE ** (-2.0 * np.arange(half) / HD), 2).astype(np.float32)[None]

    def vmem(*shape, dtype=BF):
        return pltpu.VMEM(shape, dtype)

    inputs = in_hbm(
        lengths[None],
        jnp.asarray(frequency),
        expert_ids.T,
        route_weights.T,
        hidden_in,
        attn_gain[None],
        query_weight,
    )
    packed, turn, normed = call(
        project,
        (
            jax.ShapeDtypeStruct((rows, wide + HD), BF),
            jax.ShapeDtypeStruct((rows, 3 * HD), F32),
            jax.ShapeDtypeStruct((rows, width), BF),
        ),
        inputs,
        specs=[HBM] * 7,
        scratch=tuple(pltpu.VMEM(a.shape, a.dtype) for a in inputs)
        + (pltpu.SemaphoreType.DMA((10,)),),
        flops=2 * rows * width * wide,
        nbytes=2 * width * wide,
    )
    shape = (pages, cache_keys.shape[2], HD)
    near = gather(packed, plan[1:])
    keyval = jnp.einsum("rd,dkc->rkc", normed, keyval_weight, preferred_element_type=F32)
    new_key = keyval[:, 0]
    new_key = new_key * turn[:, :HD] + jnp.roll(new_key, half, axis=1) * turn[:, HD : 2 * HD]
    new_kv = jnp.concatenate([new_key, keyval[:, 1]], axis=1).astype(BF)
    near, new_kv = joined(near, new_kv)
    keys, values = staged(near, cache_keys.reshape(shape), cache_values.reshape(shape))
    gathered = gather(near, plan[:1])

    place = position((page_request // rows) ^ req, plan) * rows + page_request % rows
    block = jnp.arange(QPK, dtype=I32)[None, :] * all_rows
    column = (block + place[:, None]).reshape(-1)
    fill = jnp.repeat(page_fill, QPK)
    partial = call(
        attend,
        jax.ShapeDtypeStruct((all_rows, wide + HD), BF),
        (gathered, column[:, None], column[None, :], fill[:, None], keys, values),
        scratch=(
            vmem(pages * QPK, 4 * shape[1], dtype=F32),
            vmem(pages * QPK, 4 * shape[1]),
            vmem(pages * QPK, HD, dtype=F32),
        ),
        flops=4 * pages * QPK * 4 * shape[1] * HD,
        nbytes=4 * pages * shape[1] * HD,
    )
    shared_up = jnp.transpose(shared_gate_up, (1, 2, 0))
    expert_up = jnp.transpose(expert_gate_up, (0, 2, 3, 1))
    experts = expert_up.shape[0]
    early = experts // 2
    out_w, *ups = staged(partial, out_weight, *[(expert_up, e) for e in range(early)])
    came = deliver(partial[None], plan[:1])
    came, out_w, *ups = joined(came, out_w, *ups)
    ups += staged(came, *[(expert_up, e) for e in range(early, experts)])
    came = deliver(came, plan[1:])
    came, *ups = joined(came, *ups)

    keep, send = call(
        combine,
        (jax.ShapeDtypeStruct((rows, width), F32), jax.ShapeDtypeStruct((rows, width), BF)),
        (came, packed, new_kv, out_w),
        flops=2 * rows * wide * width,
        nbytes=2 * wide * width,
        mib=8,
    )
    keep = keep + swap(send, 0, 1).astype(F32)
    sent = keep.astype(BF)
    (shared_down,) = staged(sent, shared_down)
    residual = keep + hidden_in.astype(F32)
    for i in range(1, far):
        residual = residual + swap(sent, 0, 2 * i).astype(F32)
    residual, shared_down = joined(residual, shared_down)

    (gate_w,) = staged(residual, (shared_up, 0))
    core = turn[:, 2 * HD : 2 * HD + 1]
    half_width = width // 2
    low = residual.astype(BF)
    sides = (low[:, :half_width], low[:, half_width:])
    here = trade(
        jnp.concatenate(sides, axis=0), jnp.where(core > 0.5, sides[1], sides[0]), plan[-1][0]
    )
    here = gather(here, plan[1:-1])
    here, late, gate_w = joined(here, residual, gate_w)
    there = swap(here, 1)
    here_other = swap(here, 0, 1)
    shared = call(
        shared_kernel,
        jax.ShapeDtypeStruct((rows, width), F32),
        (late, moe_gain[None], gate_w, shared_down) + in_hbm(shared_up),
        specs=[VMEM] * 4 + [HBM],
        scratch=(vmem(*shared_down.shape), pltpu.SemaphoreType.DMA((1,))),
        flops=6 * rows * width * shared_down.shape[0],
        nbytes=6 * width * shared_down.shape[0],
        mib=12,
    )
    there, shared = joined(there, shared)
    there_other = swap(there, 0, 1)

    small = (here, there, here_other, there_other, moe_gain[None], gathered[:, wide:], shared)
    blocks = (far, all_rows, quarter)
    send, acts, down = call(
        functools.partial(experts_kernel, top, experts),
        (
            jax.ShapeDtypeStruct(blocks, BF),
            jax.ShapeDtypeStruct((experts, all_rows, expert_down.shape[1]), BF),
            pltpu.VMEM(expert_down.shape, BF),
        ),
        small + tuple(ups) + in_hbm(expert_down),
        specs=[VMEM] * (7 + experts) + [HBM],
        scratch=(
            vmem(all_rows, width),
            vmem(all_rows, HD, dtype=F32),
            pltpu.SemaphoreType.DMA((experts,)),
        ),
        flops=5 * all_rows * width * 2 * expert_down.shape[1],
        nbytes=5 * width * 2 * expert_down.shape[1],
    )
    keep = call(
        keep_kernel,
        jax.ShapeDtypeStruct(blocks, F32),
        (acts, down, shared),
        flops=all_rows * width * 2 * expert_down.shape[1],
        nbytes=width * 2 * expert_down.shape[1],
        mib=16,
    )
    keep = keep + swap(send, 0, 1).astype(F32)
    part = all_rows // 2
    total = keep[0, :part]
    for i in reversed(range(far)):
        for j in (1, 0):
            if i or j:
                sent = keep[i, j * part : (j + 1) * part].astype(BF)
                total = total + swap(sent, j, 2 * i).astype(F32)
    total = scatter(total, plan[1:])
    own = lax.dynamic_slice_in_dim(residual, index_of(HEAD) * quarter, quarter, 1)
    return (own + total).astype(BF)


def solution(mesh):
    in_specs = (
        P("req", None),
        P("req"),
        P("req"),
        P("req"),
        P("req", "head", None, None),
        P("req", "head", None, None),
        P(),
        P(None, "head"),
        P(None, None, "head"),
        P("head", None),
        P(),
        P(None, None, "head"),
        P("head", None),
        P("req", None, None, "head"),
        P("req", "head", None),
        P("req", None),
        P("req", None),
    )
    out_specs = P("req", "head")
    shape = (mesh.shape["req"] // 2, 2, mesh.shape["head"] // 2, 2)
    split = Mesh(mesh.devices.reshape(shape), REQ + HEAD)
    names = {"req": REQ, "head": HEAD}
    in_specs, out_specs = jax.tree.map(
        lambda spec: P(*(names.get(n) for n in spec)),
        (in_specs, out_specs),
        is_leaf=lambda spec: isinstance(spec, P),
    )
    return jax.shard_map(local, mesh=split, in_specs=in_specs, out_specs=out_specs, check_vma=False)
```

time: 217 us -> 68.2 us (0.31)
  blocking collectives: 56.8 us -> 0 us
  waiting for transfers between devices: 72 us -> 16.7 us
  matrix products: 29.3 us -> 0.25 us
  Pallas kernels: 0 us -> 21 us
  local copies, waits for them, and re-layouts: 14.7 us -> 0.53 us
  between operations: 13.7 us -> 0.24 us
  other arithmetic: 10.7 us -> 1.24 us
  starting transfers between devices: 18.9 us -> 28 us
    all_gather x1 -> x0, blocking collectives: 32.3 us -> none  [local(): lax.all_gather(query_local.reshape(rows_here, query_heads * HD), 'req', a...]
    dot_general x15 -> x1, matrix products: 29.3 us -> 0.25 us  [local(): jnp.einsum('rd,dkc->rkc', normed, keyval_weight, preferred_element_type=F32)]
    psum x1 -> x0, waiting for transfers between devices: 28.6 us -> none  [local(): lax.psum(jnp.dot(attention, out_weight, preferred_element_type=jnp.float3...]
    ppermute x0 -> x22, starting transfers between devices: none -> 28 us  [the longest x21 26.3 us: swap(): lax.ppermute(value, REQ + HEAD, [(i, i ^ step) for i in range(count)])]
    all_to_all x4 -> x0, waiting for transfers between devices: 25.4 us -> none  [the longest x1 13.6 us: local(): lax.all_to_all(result.astype(jnp.bfloat16), 'req', split_axis=0, concat_a...]
    all_to_all x1 -> x0, blocking collectives: 24.5 us -> none  [local(): lax.all_to_all(outgoing, 'req', split_axis=0, concat_axis=0, tiled=True)]
    pallas_call x0 -> x11, Pallas kernels: none -> 21 us  [call(): pl.pallas_call(kernel, out_shape=out_shape, in_specs=specs or [VMEM] * le...]
    all_to_all x4 -> x0, starting transfers between devices: 18.6 us -> none  [the longest x1 5.51 us: local(): lax.all_to_all(cache_max.reshape(req_count, rows_here, query_heads), 'req...]
  transfers between devices with their start and end apart: 6 -> 22, of which waited for: 6 -> 17; matrix products, arithmetic and copies ran while one was open for 7% -> 1% of each run, Pallas kernels for 0% -> 21%
where the time goes in v1:
time: 68.2 us; the launch traced here: 67.9 us
  starting transfers between devices  28 us (41%)
  Pallas kernels  21 us (31%)
  waiting for transfers between devices  16.7 us (24%)
  other arithmetic  1.24 us (2%)
    ppermute x21, starting transfers between devices, swap(): lax.ppermute(value, REQ + HEAD, [(i, i ^ step) for i in range(count)])  26.3 us
    pallas_call x11, Pallas kernels, call(): pl.pallas_call(kernel, out_shape=out_shape, in_specs=specs or [VMEM] * le...  21 us
    ppermute x21, waiting for transfers between devices, swap(): lax.ppermute(value, REQ + HEAD, [(i, i ^ step) for i in range(count)])  16.7 us
    ppermute x1, starting transfers between devices, trade(): lax.ppermute(whole, REQ + HEAD, [(i, i ^ steps[i % 2]) for i in range(cou...  1.65 us
  transfers between devices with their start and end apart: 22, of which 17 were waited for; matrix products, arithmetic and copies ran while one was open for 1% of the time, Pallas kernels for 21%

profile of v1, /device:TPU:0, one launch (start us, length us, event | category | flops | bytes accessed | tf_op | source)
XLA Modules:
  0.0 67.9 jit_solution(8447036471032627993)
XLA Ops:
  0.0 2.4 %shard_map.172 = (bf16[16,640]{1,0:T(8,128)(2,1)S(1)}, f32[16,384]{1,0:T(8,128)S(1)}, bf16[16,2048]{1,0:T(8,128)(2,1)S(1)}) custom-call(s32[1,16]{1,0:T(1,128)} %bitcast.46, f32[1,128]{1,0:T(1,128)} %constant.61.clone.freq_hbm, s32[6,16]{1,0:T(8,128)} %bitcast.44, f32[6,16]{1,0:T(8,128)} %bitcast.45, bf16[16,2048]{1,0:T(8,128)(2,1)} %hidden_hbm.1, ...), custom_call_target="tpu_custom_call" | custom-call | flops 33554432 | bytes 2097152 | tf_op jit(solution)/shard_map/pallas_call | solution.py:114
  2.4 5.1 %collective-permute-start.2 = (bf16[16,640]{1,0:T(8,128)(2,1)S(1)}, bf16[16,640]{1,0:T(8,128)(2,1)S(1)}, u32[]{:S(2)}, u32[]{:S(2)}) collective-permute-start(bf16[16,640]{1,0:T(8,128)(2,1)S(1)} %get-tuple-element.32.query_ref), channel_id=1, source_target_pairs={{0,24},{1,25},{2,26},{3,27},{4,28},{5,29},{6,30},{7,31},{8,16},{9,... | collective-permute-start | bytes 61448 | tf_op jit(solution)/shard_map/ppermute | solution.py:50
  7.5 0.6 collective-permute-start
  8.2 0.2 fusion
  9.1 0.2 collective-permute-done.2
  9.3 2.9 %collective-permute-done.1 = bf16[16,640]{1,0:T(8,128)(2,1)S(1)} collective-permute-done((bf16[16,640]{1,0:T(8,128)(2,1)S(1)}, bf16[16,640]{1,0:T(8,128)(2,1)S(1)}, u32[]{:S(2)}, u32[]{:S(2)}) %collective-permute-start.1) | collective-permute-done | bytes 20512 | tf_op jit(solution)/shard_map/ppermute | solution.py:50
  12.2 1.6 %collective-permute-start.3 = (bf16[64,640]{1,0:T(8,128)(2,1)S(1)}, bf16[64,640]{1,0:T(8,128)(2,1)S(1)}, u32[]{:S(2)}, u32[]{:S(2)}) collective-permute-start(bf16[64,640]{1,0:T(8,128)(2,1)S(1)} %pad_maximum_fusion.3.refs_0_), channel_id=1, source_target_pairs={{0,4},{1,5},{2,6},{3,7},{4,0},{5,1},{6,2},{7,3},{8,12},{9,13},{10,... | collective-permute-start | bytes 245768 | tf_op jit(solution)/shard_map/ppermute | solution.py:50
  13.8 2.2 %shard_map.173 = (bf16[64,128,128]{2,1,0:T(8,128)(2,1)S(1)}, bf16[64,128,128]{2,1,0:T(8,128)(2,1)S(1)}) custom-call(bf16[64,640]{1,0:T(8,128)(2,1)S(1)} %pad_maximum_fusion.3.refs_0_, bf16[64,128,128]{2,1,0:T(8,128)(2,1)} %bitcast.41, bf16[64,128,128]{2,1,0:T(8,128)(2,1)} %bitcast.42), custom_call_target="tpu_custom_call" | custom-call | bytes 4194304 | tf_op jit(solution)/shard_map/pallas_call | solution.py:114
  16.1 0.7 collective-permute-done.3
  16.7 1.4 %shard_map.174.refs_0_ = bf16[128,640]{1,0:T(8,128)(2,1)S(1)} custom-call(bf16[128,640]{1,0:T(8,128)(2,1)S(1)} %constant_dynamic-update-slice_fusion.query_ref, s32[256,1]{1,0:T(8,128)S(1)} %add.114.column_ref, s32[1,256]{1,0:T(1,128)S(1)} %add.100.row_ref, s32[256,1]{1,0:T(8,128)S(1)} %broadcast_in_dim_reshape.6.fill_ref, ...), custom_call_target="tpu_custom_call" | custom-call | flops 67108864 | bytes 4194304 | tf_op jit(solution)/shard_map/pallas_call | solution.py:114
  18.1 1.6 %collective-permute-start.4 = (bf16[1,64,640]{2,1,0:T(8,128)(2,1)S(1)}, bf16[1,64,640]{2,1,0:T(8,128)(2,1)S(1)}, u32[]{:S(2)}, u32[]{:S(2)}) collective-permute-start(bf16[1,64,640]{2,1,0:T(8,128)(2,1)S(1)} %get-tuple-element.71), channel_id=1, source_target_pairs={{0,4},{1,5},{2,6},{3,7},{4,0},{5,1},{6,2},{7,3},{8,12},{9,13},{10,... | collective-permute-start | bytes 245768 | tf_op jit(solution)/shard_map/ppermute | solution.py:50
  19.7 2.5 %shard_map.175 = (bf16[512,2048]{1,0:T(8,128)(2,1)S(1)}, bf16[2,352,2048]{2,1,0:T(8,128)(2,1)S(1)}) custom-call(bf16[128,640]{1,0:T(8,128)(2,1)S(1)} %shard_map.174.refs_0_, bf16[512,2048]{1,0:T(8,128)(2,1)} %refs_1_.2, bf16[2,2,352,2048]{3,2,1,0:T(8,128)(2,1)} %bitcast.37), custom_call_target="tpu_custom_call" | custom-call | bytes 4980736 | tf_op jit(solution)/shard_map/pallas_call | solution.py:114
  22.2 0.4 collective-permute-done.4
  22.7 1.5 %collective-permute-start.7 = (bf16[2,16,640]{2,1,0:T(8,128)(2,1)S(1)}, bf16[2,16,640]{2,1,0:T(8,128)(2,1)S(1)}, u32[]{:S(2)}, u32[]{:S(2)}) collective-permute-start(bf16[2,16,640]{2,1,0:T(8,128)(2,1)S(1)} %get-tuple-element.67), channel_id=1, source_target_pairs={{0,24},{1,25},{2,26},{3,27},{4,28},{5,29},{6,30},{7,31},{8,16},{9,... | collective-permute-start | bytes 122888 | tf_op jit(solution)/shard_map/ppermute | solution.py:50
  24.2 0.6 collective-permute-start.6
  24.9 2.3 %collective-permute-start.5 = (bf16[2,16,640]{2,1,0:T(8,128)(2,1)S(1)}, bf16[2,16,640]{2,1,0:T(8,128)(2,1)S(1)}, u32[]{:S(2)}, u32[]{:S(2)}) collective-permute-start(bf16[2,16,640]{2,1,0:T(8,128)(2,1)S(1)} %get-tuple-element.69), channel_id=1, source_target_pairs={{0,8},{1,9},{2,10},{3,11},{4,12},{5,13},{6,14},{7,15},{8,0},{9,1},... | collective-permute-start | bytes 122888 | tf_op jit(solution)/shard_map/ppermute | solution.py:50
  27.1 1.8 %shard_map.176.refs_8_ = bf16[2,352,2048]{2,1,0:T(8,128)(2,1)S(1)} custom-call(bf16[2,64,640]{2,1,0:T(8,128)(2,1)S(1)} %pad_maximum_fusion.refs_0_, bf16[2,2,352,2048]{3,2,1,0:T(8,128)(2,1)} %bitcast.38), custom_call_target="tpu_custom_call" | custom-call | bytes 2883584 | tf_op jit(solution)/shard_map/pallas_call | solution.py:114
  29.0 0.2 collective-permute-done.6
  29.2 0.4 collective-permute-done.5
  29.6 0.6 shard_map.177
  30.2 1.3 %collective-permute-done.8 = bf16[16,2048]{1,0:T(8,128)(2,1)S(1)} collective-permute-done((bf16[16,2048]{1,0:T(8,128)(2,1)S(1)}, bf16[16,2048]{1,0:T(8,128)(2,1)S(1)}, u32[]{:S(2)}, u32[]{:S(2)}) %collective-permute-start.8) | collective-permute-done | bytes 65568 | tf_op jit(solution)/shard_map/ppermute | solution.py:50
  31.5 1.5 %collective-permute-start.9 = (bf16[16,2048]{1,0:T(8,128)(2,1)S(1)}, bf16[16,2048]{1,0:T(8,128)(2,1)S(1)}, u32[]{:S(2)}, u32[]{:S(2)}) collective-permute-start(bf16[16,2048]{1,0:T(8,128)(2,1)S(1)} %fusion.5.refs_0_), channel_id=1, source_target_pairs={{0,2},{1,3},{2,0},{3,1},{4,6},{5,7},{6,4},{7,5},{8,10},{9,11},{10,... | collective-permute-start | bytes 196616 | tf_op jit(solution)/shard_map/ppermute | solution.py:50
  33.2 1.9 %shard_map.178.down_ref = bf16[704,2048]{1,0:T(8,128)(2,1)S(1)} custom-call(bf16[16,2048]{1,0:T(8,128)(2,1)S(1)} %fusion.5.refs_0_, bf16[704,2048]{1,0:T(8,128)(2,1)} %refs_1_.3), custom_call_target="tpu_custom_call" | custom-call | bytes 2883584 | tf_op jit(solution)/shard_map/pallas_call | solution.py:114
  35.1 0.8 %collective-permute-done.9 = bf16[16,2048]{1,0:T(8,128)(2,1)S(1)} collective-permute-done((bf16[16,2048]{1,0:T(8,128)(2,1)S(1)}, bf16[16,2048]{1,0:T(8,128)(2,1)S(1)}, u32[]{:S(2)}, u32[]{:S(2)}) %collective-permute-start.9) | collective-permute-done | bytes 65568 | tf_op jit(solution)/shard_map/ppermute | solution.py:50
  36.0 1.7 %collective-permute-start.10 = (bf16[32,1024]{1,0:T(8,128)(2,1)S(1)}, bf16[32,1024]{1,0:T(8,128)(2,1)S(1)}, u32[]{:S(2)}, u32[]{:S(2)}) collective-permute-start(bf16[32,1024]{1,0:T(8,128)(2,1)S(1)} %pad_maximum_fusion.4), channel_id=1, source_target_pairs={{0,16},{1,25},{2,18},{3,27},{4,20},{5,29},{6,22},{7,31},{8,24},{9,... | collective-permute-start | bytes 196616 | tf_op jit(solution)/shard_map/ppermute | solution.py:67
  37.6 1.3 %collective-permute-start.11 = (bf16[16,1024]{1,0:T(8,128)(2,1)S(1)}, bf16[16,1024]{1,0:T(8,128)(2,1)S(1)}, u32[]{:S(2)}, u32[]{:S(2)}) collective-permute-start(bf16[16,1024]{1,0:T(8,128)(2,1)S(1)} %get-tuple-element.76), channel_id=1, source_target_pairs={{0,8},{1,9},{2,10},{3,11},{4,12},{5,13},{6,14},{7,15},{8,0},{9,1},... | collective-permute-start | bytes 98312 | tf_op jit(solution)/shard_map/ppermute | solution.py:50
  39.0 1.8 %shard_map.179.gate_ref = bf16[704,2048]{1,0:T(8,128)(2,1)S(1)} custom-call(f32[16,2048]{1,0:T(8,128)S(1)} %convert_add_fusion.1.refs_0_.residual_ref, bf16[2,704,2048]{2,1,0:T(8,128)(2,1)} %bitcast.39), custom_call_target="tpu_custom_call" | custom-call | bytes 2883584 | tf_op jit(solution)/shard_map/pallas_call | solution.py:114
  40.8 0.8 %collective-permute-done.11 = bf16[16,1024]{1,0:T(8,128)(2,1)S(1)} collective-permute-done((bf16[16,1024]{1,0:T(8,128)(2,1)S(1)}, bf16[16,1024]{1,0:T(8,128)(2,1)S(1)}, u32[]{:S(2)}, u32[]{:S(2)}) %collective-permute-start.11) | collective-permute-done | bytes 32800 | tf_op jit(solution)/shard_map/ppermute | solution.py:50
  41.7 1.6 %collective-permute-start.12 = (bf16[64,1024]{1,0:T(8,128)(2,1)S(1)}, bf16[64,1024]{1,0:T(8,128)(2,1)S(1)}, u32[]{:S(2)}, u32[]{:S(2)}) collective-permute-start(bf16[64,1024]{1,0:T(8,128)(2,1)S(1)} %pad_maximum_fusion.2.refs_0_), channel_id=1, source_target_pairs={{0,4},{1,5},{2,6},{3,7},{4,0},{5,1},{6,2},{7,3},{8,12},{9,13},{10,... | collective-permute-start | bytes 393224 | tf_op jit(solution)/shard_map/ppermute | solution.py:50
  43.3 3.3 %shard_map.180.refs_6_.shared_ref = f32[16,2048]{1,0:T(8,128)S(1)} custom-call(f32[16,2048]{1,0:T(8,128)S(1)} %convert_add_fusion.1.refs_0_.residual_ref, f32[1,2048]{1,0:T(1,128)S(1)} %bitcast.35, bf16[704,2048]{1,0:T(8,128)(2,1)S(1)} %shard_map.179.gate_ref, bf16[704,2048]{1,0:T(8,128)(2,1)S(1)} %shard_map.178.down_ref, bf16[2,704,2048]{2,1,0:T(8,128)(2,1)} %bitcast.40), custom_call_target="tpu_custom_call" | custom-call | flops 138412032 | bytes 8650752 | tf_op jit(solution)/shard_map/pallas_call | solution.py:114
  46.6 0.4 collective-permute-done.12.refs_1_
  46.9 0.2 collective-permute-start.14
  47.1 1.1 %collective-permute-done.14.refs_3_ = bf16[64,1024]{1,0:T(8,128)(2,1)S(1)} collective-permute-done((bf16[64,1024]{1,0:T(8,128)(2,1)S(1)}, bf16[64,1024]{1,0:T(8,128)(2,1)S(1)}, u32[]{:S(2)}, u32[]{:S(2)}) %collective-permute-start.14) | collective-permute-done | bytes 131104 | tf_op jit(solution)/shard_map/ppermute | solution.py:50
  48.3 2.6 %shard_map.181 = (bf16[2,128,512]{2,1,0:T(8,128)(2,1)S(1)}, bf16[2,128,352]{2,1,0:T(8,128)(2,1)S(1)}, bf16[2,352,2048]{2,1,0:T(8,128)(2,1)S(1)}) custom-call(bf16[64,1024]{1,0:T(8,128)(2,1)S(1)} %pad_maximum_fusion.2.refs_0_, bf16[64,1024]{1,0:T(8,128)(2,1)S(1)} %collective-permute-done.12.refs_1_, bf16[64,1024]{1,0:T(8,128)(2,1)S(1)} %collective-permute-done.13.refs_2_, ...), custom_call_target="tpu_custom_call" | custom-call | flops 922746880 | bytes 7208960 | tf_op jit(solution)/shard_map/pallas_call | solution.py:114
  50.9 0.3 collective-permute-start.15
  51.2 0.4 shard_map.182
  51.6 0.9 %collective-permute-done.15 = bf16[2,128,512]{2,1,0:T(8,128)(2,1)S(1)} collective-permute-done((bf16[2,128,512]{2,1,0:T(8,128)(2,1)S(1)}, bf16[2,128,512]{2,1,0:T(8,128)(2,1)S(1)}, u32[]{:S(2)}, u32[]{:S(2)}) %collective-permute-start.15) | collective-permute-done | bytes 262176 | tf_op jit(solution)/shard_map/ppermute | solution.py:50
  52.6 2.2 %collective-permute-start.16 = (bf16[64,512]{1,0:T(8,128)(2,1)S(1)}, bf16[64,512]{1,0:T(8,128)(2,1)S(1)}, u32[]{:S(2)}, u32[]{:S(2)}) collective-permute-start(bf16[64,512]{1,0:T(8,128)(2,1)S(1)} %get-tuple-element.63), channel_id=1, source_target_pairs={{0,6},{1,7},{2,4},{3,5},{4,2},{5,3},{6,0},{7,1},{8,14},{9,15},{10,... | collective-permute-start | bytes 196616 | tf_op jit(solution)/shard_map/ppermute | solution.py:50
  54.8 0.6 collective-permute-start.18
  55.4 0.8 %collective-permute-start.17 = (bf16[64,512]{1,0:T(8,128)(2,1)S(1)}, bf16[64,512]{1,0:T(8,128)(2,1)S(1)}, u32[]{:S(2)}, u32[]{:S(2)}) collective-permute-start(bf16[64,512]{1,0:T(8,128)(2,1)S(1)} %get-tuple-element.65), channel_id=1, source_target_pairs={{0,2},{1,3},{2,0},{3,1},{4,6},{5,7},{6,4},{7,5},{8,10},{9,11},{10,... | collective-permute-start | bytes 196616 | tf_op jit(solution)/shard_map/ppermute | solution.py:50
  56.2 1.7 %collective-permute-done.16 = bf16[64,512]{1,0:T(8,128)(2,1)S(1)} collective-permute-done((bf16[64,512]{1,0:T(8,128)(2,1)S(1)}, bf16[64,512]{1,0:T(8,128)(2,1)S(1)}, u32[]{:S(2)}, u32[]{:S(2)}) %collective-permute-start.16) | collective-permute-done | bytes 65568 | tf_op jit(solution)/shard_map/ppermute | solution.py:50
  57.9 1.3 %collective-permute-done.18 = bf16[64,512]{1,0:T(8,128)(2,1)S(1)} collective-permute-done((bf16[64,512]{1,0:T(8,128)(2,1)S(1)}, bf16[64,512]{1,0:T(8,128)(2,1)S(1)}, u32[]{:S(2)}, u32[]{:S(2)}) %collective-permute-start.18) | collective-permute-done | bytes 65568 | tf_op jit(solution)/shard_map/ppermute | solution.py:50
  59.3 0.4 collective-permute-done.17
  59.7 2.9 %collective-permute-start.19 = (bf16[16,512]{1,0:T(8,128)(2,1)S(1)}, bf16[16,512]{1,0:T(8,128)(2,1)S(1)}, u32[]{:S(2)}, u32[]{:S(2)}) collective-permute-start(bf16[16,512]{1,0:T(8,128)(2,1)S(1)} %get-tuple-element.72), channel_id=1, source_target_pairs={{0,24},{1,25},{2,26},{3,27},{4,28},{5,29},{6,30},{7,31},{8,16},{9,... | collective-permute-start | bytes 49160 | tf_op jit(solution)/shard_map/ppermute | solution.py:50
  62.6 1.5 %collective-permute-start.20 = (bf16[16,512]{1,0:T(8,128)(2,1)S(1)}, bf16[16,512]{1,0:T(8,128)(2,1)S(1)}, u32[]{:S(2)}, u32[]{:S(2)}) collective-permute-start(bf16[16,512]{1,0:T(8,128)(2,1)S(1)} %get-tuple-element.74), channel_id=1, source_target_pairs={{0,8},{1,9},{2,10},{3,11},{4,12},{5,13},{6,14},{7,15},{8,0},{9,1},... | collective-permute-start | bytes 49160 | tf_op jit(solution)/shard_map/ppermute | solution.py:50
  64.2 1.1 %collective-permute-done.19 = bf16[16,512]{1,0:T(8,128)(2,1)S(1)} collective-permute-done((bf16[16,512]{1,0:T(8,128)(2,1)S(1)}, bf16[16,512]{1,0:T(8,128)(2,1)S(1)}, u32[]{:S(2)}, u32[]{:S(2)}) %collective-permute-start.19) | collective-permute-done | bytes 16416 | tf_op jit(solution)/shard_map/ppermute | solution.py:50
  65.3 1.9 %collective-permute-done.21 = bf16[16,512]{1,0:T(8,128)(2,1)S(1)} collective-permute-done((bf16[16,512]{1,0:T(8,128)(2,1)S(1)}, bf16[16,512]{1,0:T(8,128)(2,1)S(1)}, u32[]{:S(2)}, u32[]{:S(2)}) %collective-permute-start.21) | collective-permute-done | bytes 16416 | tf_op jit(solution)/shard_map/ppermute | solution.py:50
  67.3 0.6 fusion.10
  (50 shorter events, 1.2 us)
Async XLA Ops:
  0.0 8.2 %copy-start = (bf16[2048,2,128]{2,1,0:T(2,128)(2,1)S(1)}, bf16[2048,2,128]{2,1,0:T(2,128)(2,1)}, u32[]{:S(2)}) copy-start(bf16[2048,2,128]{2,1,0:T(2,128)(2,1)} %param.26) | copy-start | bytes 3145732
  0.0 8.5 %copy-start.4 = (s32[64]{0:T(128)S(1)}, s32[64]{0:T(128)}, u32[]{:S(2)}) copy-start(s32[64]{0:T(128)} %param.20) | copy-start | bytes 772
  0.0 8.9 %copy-start.3 = (s32[64]{0:T(128)S(1)}, s32[64]{0:T(128)}, u32[]{:S(2)}) copy-start(s32[64]{0:T(128)} %param.21) | copy-start | bytes 772
  2.4 6.9 %collective-permute-start.2 = (bf16[16,640]{1,0:T(8,128)(2,1)S(1)}, bf16[16,640]{1,0:T(8,128)(2,1)S(1)}, u32[]{:S(2)}, u32[]{:S(2)}) collective-permute-start(bf16[16,640]{1,0:T(8,128)(2,1)S(1)} %get-tuple-element.32.query_ref), channel_id=1, source_target_pairs={{0,24},{1,25},{2,26},{3,27},{4,28},{5,29},{6,30},{7,31},{8,16},{9,... | collective-permute-start | bytes 61448 | tf_op jit(solution)/shard_map/ppermute | solution.py:50
  7.5 4.7 %collective-permute-start.1 = (bf16[16,640]{1,0:T(8,128)(2,1)S(1)}, bf16[16,640]{1,0:T(8,128)(2,1)S(1)}, u32[]{:S(2)}, u32[]{:S(2)}) collective-permute-start(bf16[16,640]{1,0:T(8,128)(2,1)S(1)} %get-tuple-element.32.query_ref), channel_id=1, source_target_pairs={{0,16},{1,17},{2,18},{3,19},{4,20},{5,21},{6,22},{7,23},{8,24},{9,... | collective-permute-start | bytes 61448 | tf_op jit(solution)/shard_map/ppermute | solution.py:50
  7.5 4.7 %collective-permute-start = (bf16[16,640]{1,0:T(8,128)(2,1)S(1)}, bf16[16,640]{1,0:T(8,128)(2,1)S(1)}, u32[]{:S(2)}, u32[]{:S(2)}) collective-permute-start(bf16[16,640]{1,0:T(8,128)(2,1)S(1)} %get-tuple-element.32.query_ref), channel_id=1, source_target_pairs={{0,8},{1,9},{2,10},{3,11},{4,12},{5,13},{6,14},{7,15},{8,0},{9,1},... | collective-permute-start | bytes 61448 | tf_op jit(solution)/shard_map/ppermute | solution.py:50
  12.2 4.5 %collective-permute-start.3 = (bf16[64,640]{1,0:T(8,128)(2,1)S(1)}, bf16[64,640]{1,0:T(8,128)(2,1)S(1)}, u32[]{:S(2)}, u32[]{:S(2)}) collective-permute-start(bf16[64,640]{1,0:T(8,128)(2,1)S(1)} %pad_maximum_fusion.3.refs_0_), channel_id=1, source_target_pairs={{0,4},{1,5},{2,6},{3,7},{4,0},{5,1},{6,2},{7,3},{8,12},{9,13},{10,... | collective-permute-start | bytes 245768 | tf_op jit(solution)/shard_map/ppermute | solution.py:50
  18.1 4.5 %collective-permute-start.4 = (bf16[1,64,640]{2,1,0:T(8,128)(2,1)S(1)}, bf16[1,64,640]{2,1,0:T(8,128)(2,1)S(1)}, u32[]{:S(2)}, u32[]{:S(2)}) collective-permute-start(bf16[1,64,640]{2,1,0:T(8,128)(2,1)S(1)} %get-tuple-element.71), channel_id=1, source_target_pairs={{0,4},{1,5},{2,6},{3,7},{4,0},{5,1},{6,2},{7,3},{8,12},{9,13},{10,... | collective-permute-start | bytes 245768 | tf_op jit(solution)/shard_map/ppermute | solution.py:50
  22.7 6.3 %collective-permute-start.7 = (bf16[2,16,640]{2,1,0:T(8,128)(2,1)S(1)}, bf16[2,16,640]{2,1,0:T(8,128)(2,1)S(1)}, u32[]{:S(2)}, u32[]{:S(2)}) collective-permute-start(bf16[2,16,640]{2,1,0:T(8,128)(2,1)S(1)} %get-tuple-element.67), channel_id=1, source_target_pairs={{0,24},{1,25},{2,26},{3,27},{4,28},{5,29},{6,30},{7,31},{8,16},{9,... | collective-permute-start | bytes 122888 | tf_op jit(solution)/shard_map/ppermute | solution.py:50
  24.2 4.9 %collective-permute-start.6 = (bf16[2,16,640]{2,1,0:T(8,128)(2,1)S(1)}, bf16[2,16,640]{2,1,0:T(8,128)(2,1)S(1)}, u32[]{:S(2)}, u32[]{:S(2)}) collective-permute-start(bf16[2,16,640]{2,1,0:T(8,128)(2,1)S(1)} %get-tuple-element.68), channel_id=1, source_target_pairs={{0,16},{1,17},{2,18},{3,19},{4,20},{5,21},{6,22},{7,23},{8,24},{9,... | collective-permute-start | bytes 122888 | tf_op jit(solution)/shard_map/ppermute | solution.py:50
  24.9 4.7 %collective-permute-start.5 = (bf16[2,16,640]{2,1,0:T(8,128)(2,1)S(1)}, bf16[2,16,640]{2,1,0:T(8,128)(2,1)S(1)}, u32[]{:S(2)}, u32[]{:S(2)}) collective-permute-start(bf16[2,16,640]{2,1,0:T(8,128)(2,1)S(1)} %get-tuple-element.69), channel_id=1, source_target_pairs={{0,8},{1,9},{2,10},{3,11},{4,12},{5,13},{6,14},{7,15},{8,0},{9,1},... | collective-permute-start | bytes 122888 | tf_op jit(solution)/shard_map/ppermute | solution.py:50
  30.2 1.3 %collective-permute-start.8 = (bf16[16,2048]{1,0:T(8,128)(2,1)S(1)}, bf16[16,2048]{1,0:T(8,128)(2,1)S(1)}, u32[]{:S(2)}, u32[]{:S(2)}) collective-permute-start(bf16[16,2048]{1,0:T(8,128)(2,1)S(1)} %get-tuple-element.46), channel_id=1, source_target_pairs={{0,1},{1,0},{2,3},{3,2},{4,5},{5,4},{6,7},{7,6},{8,9},{9,8},{10,11... | collective-permute-start | bytes 196616 | tf_op jit(solution)/shard_map/ppermute | solution.py:50
  31.5 4.3 %collective-permute-start.9 = (bf16[16,2048]{1,0:T(8,128)(2,1)S(1)}, bf16[16,2048]{1,0:T(8,128)(2,1)S(1)}, u32[]{:S(2)}, u32[]{:S(2)}) collective-permute-start(bf16[16,2048]{1,0:T(8,128)(2,1)S(1)} %fusion.5.refs_0_), channel_id=1, source_target_pairs={{0,2},{1,3},{2,0},{3,1},{4,6},{5,7},{6,4},{7,5},{8,10},{9,11},{10,... | collective-permute-start | bytes 196616 | tf_op jit(solution)/shard_map/ppermute | solution.py:50
  33.2 2.7 %copy-start.2 = (bf16[16,2048]{1,0:T(8,128)(2,1)S(1)}, bf16[16,2048]{1,0:T(8,128)(2,1)}, u32[]{:S(2)}) copy-start(bf16[16,2048]{1,0:T(8,128)(2,1)} %hidden_hbm.1) | copy-start | bytes 196612
  36.0 5.7 %collective-permute-start.10 = (bf16[32,1024]{1,0:T(8,128)(2,1)S(1)}, bf16[32,1024]{1,0:T(8,128)(2,1)S(1)}, u32[]{:S(2)}, u32[]{:S(2)}) collective-permute-start(bf16[32,1024]{1,0:T(8,128)(2,1)S(1)} %pad_maximum_fusion.4), channel_id=1, source_target_pairs={{0,16},{1,25},{2,18},{3,27},{4,20},{5,29},{6,22},{7,31},{8,24},{9,... | collective-permute-start | bytes 196616 | tf_op jit(solution)/shard_map/ppermute | solution.py:67
  37.6 4.0 %collective-permute-start.11 = (bf16[16,1024]{1,0:T(8,128)(2,1)S(1)}, bf16[16,1024]{1,0:T(8,128)(2,1)S(1)}, u32[]{:S(2)}, u32[]{:S(2)}) collective-permute-start(bf16[16,1024]{1,0:T(8,128)(2,1)S(1)} %get-tuple-element.76), channel_id=1, source_target_pairs={{0,8},{1,9},{2,10},{3,11},{4,12},{5,13},{6,14},{7,15},{8,0},{9,1},... | collective-permute-start | bytes 98312 | tf_op jit(solution)/shard_map/ppermute | solution.py:50
  39.0 4.3 %copy-start.1 = (f32[2048]{0:T(1024)S(1)}, f32[2048]{0:T(1024)}, u32[]{:S(2)}) copy-start(f32[2048]{0:T(1024)} %param.28) | copy-start | bytes 24580
  41.7 5.3 %collective-permute-start.12 = (bf16[64,1024]{1,0:T(8,128)(2,1)S(1)}, bf16[64,1024]{1,0:T(8,128)(2,1)S(1)}, u32[]{:S(2)}, u32[]{:S(2)}) collective-permute-start(bf16[64,1024]{1,0:T(8,128)(2,1)S(1)} %pad_maximum_fusion.2.refs_0_), channel_id=1, source_target_pairs={{0,4},{1,5},{2,6},{3,7},{4,0},{5,1},{6,2},{7,3},{8,12},{9,13},{10,... | collective-permute-start | bytes 393224 | tf_op jit(solution)/shard_map/ppermute | solution.py:50
  43.3 3.9 %collective-permute-start.13 = (bf16[64,1024]{1,0:T(8,128)(2,1)S(1)}, bf16[64,1024]{1,0:T(8,128)(2,1)S(1)}, u32[]{:S(2)}, u32[]{:S(2)}) collective-permute-start(bf16[64,1024]{1,0:T(8,128)(2,1)S(1)} %pad_maximum_fusion.2.refs_0_), channel_id=1, source_target_pairs={{0,1},{1,0},{2,3},{3,2},{4,5},{5,4},{6,7},{7,6},{8,9},{9,8},{10,11... | collective-permute-start | bytes 393224 | tf_op jit(solution)/shard_map/ppermute | solution.py:50
  46.9 1.3 %collective-permute-start.14 = (bf16[64,1024]{1,0:T(8,128)(2,1)S(1)}, bf16[64,1024]{1,0:T(8,128)(2,1)S(1)}, u32[]{:S(2)}, u32[]{:S(2)}) collective-permute-start(bf16[64,1024]{1,0:T(8,128)(2,1)S(1)} %collective-permute-done.12.refs_1_), channel_id=1, source_target_pairs={{0,1},{1,0},{2,3},{3,2},{4,5},{5,4},{6,7},{7,6},{8,9},{9,8},{10,11... | collective-permute-start | bytes 393224 | tf_op jit(solution)/shard_map/ppermute | solution.py:50
  50.9 1.6 %collective-permute-start.15 = (bf16[2,128,512]{2,1,0:T(8,128)(2,1)S(1)}, bf16[2,128,512]{2,1,0:T(8,128)(2,1)S(1)}, u32[]{:S(2)}, u32[]{:S(2)}) collective-permute-start(bf16[2,128,512]{2,1,0:T(8,128)(2,1)S(1)} %get-tuple-element.58), channel_id=1, source_target_pairs={{0,1},{1,0},{2,3},{3,2},{4,5},{5,4},{6,7},{7,6},{8,9},{9,8},{10,11... | collective-permute-start | bytes 786440 | tf_op jit(solution)/shard_map/ppermute | solution.py:50
  52.6 5.3 %collective-permute-start.16 = (bf16[64,512]{1,0:T(8,128)(2,1)S(1)}, bf16[64,512]{1,0:T(8,128)(2,1)S(1)}, u32[]{:S(2)}, u32[]{:S(2)}) collective-permute-start(bf16[64,512]{1,0:T(8,128)(2,1)S(1)} %get-tuple-element.63), channel_id=1, source_target_pairs={{0,6},{1,7},{2,4},{3,5},{4,2},{5,3},{6,0},{7,1},{8,14},{9,15},{10,... | collective-permute-start | bytes 196616 | tf_op jit(solution)/shard_map/ppermute | solution.py:50
  54.8 4.4 %collective-permute-start.18 = (bf16[64,512]{1,0:T(8,128)(2,1)S(1)}, bf16[64,512]{1,0:T(8,128)(2,1)S(1)}, u32[]{:S(2)}, u32[]{:S(2)}) collective-permute-start(bf16[64,512]{1,0:T(8,128)(2,1)S(1)} %get-tuple-element.64), channel_id=1, source_target_pairs={{0,4},{1,5},{2,6},{3,7},{4,0},{5,1},{6,2},{7,3},{8,12},{9,13},{10,... | collective-permute-start | bytes 196616 | tf_op jit(solution)/shard_map/ppermute | solution.py:50
  55.4 4.3 %collective-permute-start.17 = (bf16[64,512]{1,0:T(8,128)(2,1)S(1)}, bf16[64,512]{1,0:T(8,128)(2,1)S(1)}, u32[]{:S(2)}, u32[]{:S(2)}) collective-permute-start(bf16[64,512]{1,0:T(8,128)(2,1)S(1)} %get-tuple-element.65), channel_id=1, source_target_pairs={{0,2},{1,3},{2,0},{3,1},{4,6},{5,7},{6,4},{7,5},{8,10},{9,11},{10,... | collective-permute-start | bytes 196616 | tf_op jit(solution)/shard_map/ppermute | solution.py:50
  59.7 5.6 %collective-permute-start.19 = (bf16[16,512]{1,0:T(8,128)(2,1)S(1)}, bf16[16,512]{1,0:T(8,128)(2,1)S(1)}, u32[]{:S(2)}, u32[]{:S(2)}) collective-permute-start(bf16[16,512]{1,0:T(8,128)(2,1)S(1)} %get-tuple-element.72), channel_id=1, source_target_pairs={{0,24},{1,25},{2,26},{3,27},{4,28},{5,29},{6,30},{7,31},{8,16},{9,... | collective-permute-start | bytes 49160 | tf_op jit(solution)/shard_map/ppermute | solution.py:50
  62.6 4.6 %collective-permute-start.21 = (bf16[16,512]{1,0:T(8,128)(2,1)S(1)}, bf16[16,512]{1,0:T(8,128)(2,1)S(1)}, u32[]{:S(2)}, u32[]{:S(2)}) collective-permute-start(bf16[16,512]{1,0:T(8,128)(2,1)S(1)} %get-tuple-element.73), channel_id=1, source_target_pairs={{0,16},{1,17},{2,18},{3,19},{4,20},{5,21},{6,22},{7,23},{8,24},{9,... | collective-permute-start | bytes 49160 | tf_op jit(solution)/shard_map/ppermute | solution.py:50
  62.6 4.6 %collective-permute-start.20 = (bf16[16,512]{1,0:T(8,128)(2,1)S(1)}, bf16[16,512]{1,0:T(8,128)(2,1)S(1)}, u32[]{:S(2)}, u32[]{:S(2)}) collective-permute-start(bf16[16,512]{1,0:T(8,128)(2,1)S(1)} %get-tuple-element.74), channel_id=1, source_target_pairs={{0,8},{1,9},{2,10},{3,11},{4,12},{5,13},{6,14},{7,15},{8,0},{9,1},... | collective-permute-start | bytes 49160 | tf_op jit(solution)/shard_map/ppermute | solution.py:50

commit v2 on v1

--- a/solution.py
+++ b/solution.py
@@ -103,7 +103,7 @@
     for shift, size in plan:
         part = blocks.shape[0] // size
         total = blocks[:part]
-        for i in (size - 1, *range(1, size - 1)):
+        for i in range(1, size):
             sent = blocks[i * part : (i + 1) * part].astype(BF)
             total = total + swap(sent, i << shift).astype(F32)
         blocks = total
@@ -180,19 +180,18 @@
     chunks = sem.shape[0] - 6
     deep = weight.shape[0] // chunks
     parts = [pl.ds(i * deep, deep) for i in range(chunks)]
-    *heavy, early, late, first, second, third, last = fetch(
-        [(weight_hbm.at[p], weight.at[p]) for p in parts]
-        + [
+    copies = fetch(
+        [
             (lengths_hbm, lengths),
             (freq_hbm, freq),
             (ids_hbm, ids),
             (route_hbm, routes),
             (hidden_hbm, hidden),
             (gain_hbm, gain),
-        ],
+        ]
+        + [(weight_hbm.at[p], weight.at[p]) for p in parts],
         sem,
     )
-    copies = [early, late, first, second, third, last, *heavy]
     width = weight.shape[1]
     rows = hidden.shape[0]
     copies[0].wait()
@@ -575,8 +574,8 @@
     keep = keep + swap(send, 0, 1).astype(F32)
     part = all_rows // 2
     total = keep[0, :part]
-    for i in reversed(range(far)):
-        for j in (1, 0):
+    for i in range(far):
+        for j in range(2):
             if i or j:
                 sent = keep[i, j * part : (j + 1) * part].astype(BF)
                 total = total + swap(sent, j, 2 * i).astype(F32)

time: 68.2 us -> 68.1 us (level)
  waiting for transfers between devices: 16.7 us -> 17.8 us
  starting transfers between devices: 28 us -> 27.1 us
    ppermute x21, waiting for transfers between devices: 16.7 us -> 17.8 us  [swap(): lax.ppermute(value, REQ + HEAD, [(i, i ^ step) for i in range(count)])]
    ppermute x21, starting transfers between devices: 26.3 us -> 25.4 us  [swap(): lax.ppermute(value, REQ + HEAD, [(i, i ^ step) for i in range(count)])]
where the time goes in v2:
time: 68.1 us; the launch traced here: 67.8 us
  starting transfers between devices  27.1 us (40%)
  Pallas kernels  20.6 us (30%)
  waiting for transfers between devices  17.8 us (26%)
  other arithmetic  1.24 us (2%)
    ppermute x21, starting transfers between devices, swap(): lax.ppermute(value, REQ + HEAD, [(i, i ^ step) for i in range(count)])  25.4 us
    pallas_call x11, Pallas kernels, call(): pl.pallas_call(kernel, out_shape=out_shape, in_specs=specs or [VMEM] * le...  20.6 us
    ppermute x21, waiting for transfers between devices, swap(): lax.ppermute(value, REQ + HEAD, [(i, i ^ step) for i in range(count)])  17.8 us
    ppermute x1, starting transfers between devices, trade(): lax.ppermute(whole, REQ + HEAD, [(i, i ^ steps[i % 2]) for i in range(cou...  1.66 us
  transfers between devices with their start and end apart: 22, of which 17 were waited for; matrix products, arithmetic and copies ran while one was open for 1% of the time, Pallas kernels for 21%

profile of v2, /device:TPU:0, one launch (start us, length us, event | category | flops | bytes accessed | tf_op | source)
XLA Modules:
  0.0 67.8 jit_solution(7104873524376491579)
XLA Ops:
  0.0 2.0 %shard_map.172 = (bf16[16,640]{1,0:T(8,128)(2,1)S(1)}, f32[16,384]{1,0:T(8,128)S(1)}, bf16[16,2048]{1,0:T(8,128)(2,1)S(1)}) custom-call(s32[1,16]{1,0:T(1,128)} %bitcast.46, f32[1,128]{1,0:T(1,128)} %constant.61.clone.freq_hbm, s32[6,16]{1,0:T(8,128)} %bitcast.44, f32[6,16]{1,0:T(8,128)} %bitcast.45, bf16[16,2048]{1,0:T(8,128)(2,1)} %hidden_hbm.1, ...), custom_call_target="tpu_custom_call" | custom-call | flops 33554432 | bytes 2097152 | tf_op jit(solution)/shard_map/pallas_call | solution.py:114
  2.1 5.1 %collective-permute-start.2 = (bf16[16,640]{1,0:T(8,128)(2,1)S(1)}, bf16[16,640]{1,0:T(8,128)(2,1)S(1)}, u32[]{:S(2)}, u32[]{:S(2)}) collective-permute-start(bf16[16,640]{1,0:T(8,128)(2,1)S(1)} %get-tuple-element.32.query_ref), channel_id=1, source_target_pairs={{0,24},{1,25},{2,26},{3,27},{4,28},{5,29},{6,30},{7,31},{8,16},{9,... | collective-permute-start | bytes 61448 | tf_op jit(solution)/shard_map/ppermute | solution.py:50
  7.2 0.6 collective-permute-start
  7.8 0.2 fusion
  8.7 0.2 collective-permute-done.2
  8.9 2.9 %collective-permute-done.1 = bf16[16,640]{1,0:T(8,128)(2,1)S(1)} collective-permute-done((bf16[16,640]{1,0:T(8,128)(2,1)S(1)}, bf16[16,640]{1,0:T(8,128)(2,1)S(1)}, u32[]{:S(2)}, u32[]{:S(2)}) %collective-permute-start.1) | collective-permute-done | bytes 20512 | tf_op jit(solution)/shard_map/ppermute | solution.py:50
  11.9 1.6 %collective-permute-start.3 = (bf16[64,640]{1,0:T(8,128)(2,1)S(1)}, bf16[64,640]{1,0:T(8,128)(2,1)S(1)}, u32[]{:S(2)}, u32[]{:S(2)}) collective-permute-start(bf16[64,640]{1,0:T(8,128)(2,1)S(1)} %pad_maximum_fusion.3.refs_0_), channel_id=1, source_target_pairs={{0,4},{1,5},{2,6},{3,7},{4,0},{5,1},{6,2},{7,3},{8,12},{9,13},{10,... | collective-permute-start | bytes 245768 | tf_op jit(solution)/shard_map/ppermute | solution.py:50
  13.5 2.2 %shard_map.173 = (bf16[64,128,128]{2,1,0:T(8,128)(2,1)S(1)}, bf16[64,128,128]{2,1,0:T(8,128)(2,1)S(1)}) custom-call(bf16[64,640]{1,0:T(8,128)(2,1)S(1)} %pad_maximum_fusion.3.refs_0_, bf16[64,128,128]{2,1,0:T(8,128)(2,1)} %bitcast.41, bf16[64,128,128]{2,1,0:T(8,128)(2,1)} %bitcast.42), custom_call_target="tpu_custom_call" | custom-call | bytes 4194304 | tf_op jit(solution)/shard_map/pallas_call | solution.py:114
  15.7 0.7 collective-permute-done.3
  16.4 1.4 %shard_map.174.refs_0_ = bf16[128,640]{1,0:T(8,128)(2,1)S(1)} custom-call(bf16[128,640]{1,0:T(8,128)(2,1)S(1)} %constant_dynamic-update-slice_fusion.query_ref, s32[256,1]{1,0:T(8,128)S(1)} %add.114.column_ref, s32[1,256]{1,0:T(1,128)S(1)} %add.100.row_ref, s32[256,1]{1,0:T(8,128)S(1)} %broadcast_in_dim_reshape.6.fill_ref, ...), custom_call_target="tpu_custom_call" | custom-call | flops 67108864 | bytes 4194304 | tf_op jit(solution)/shard_map/pallas_call | solution.py:114
  17.8 1.6 %collective-permute-start.4 = (bf16[1,64,640]{2,1,0:T(8,128)(2,1)S(1)}, bf16[1,64,640]{2,1,0:T(8,128)(2,1)S(1)}, u32[]{:S(2)}, u32[]{:S(2)}) collective-permute-start(bf16[1,64,640]{2,1,0:T(8,128)(2,1)S(1)} %get-tuple-element.71), channel_id=1, source_target_pairs={{0,4},{1,5},{2,6},{3,7},{4,0},{5,1},{6,2},{7,3},{8,12},{9,13},{10,... | collective-permute-start | bytes 245768 | tf_op jit(solution)/shard_map/ppermute | solution.py:50
  19.4 2.5 %shard_map.175 = (bf16[512,2048]{1,0:T(8,128)(2,1)S(1)}, bf16[2,352,2048]{2,1,0:T(8,128)(2,1)S(1)}) custom-call(bf16[128,640]{1,0:T(8,128)(2,1)S(1)} %shard_map.174.refs_0_, bf16[512,2048]{1,0:T(8,128)(2,1)} %refs_1_.2, bf16[2,2,352,2048]{3,2,1,0:T(8,128)(2,1)} %bitcast.37), custom_call_target="tpu_custom_call" | custom-call | bytes 4980736 | tf_op jit(solution)/shard_map/pallas_call | solution.py:114
  21.9 0.5 collective-permute-done.4
  22.4 1.5 %collective-permute-start.7 = (bf16[2,16,640]{2,1,0:T(8,128)(2,1)S(1)}, bf16[2,16,640]{2,1,0:T(8,128)(2,1)S(1)}, u32[]{:S(2)}, u32[]{:S(2)}) collective-permute-start(bf16[2,16,640]{2,1,0:T(8,128)(2,1)S(1)} %get-tuple-element.67), channel_id=1, source_target_pairs={{0,24},{1,25},{2,26},{3,27},{4,28},{5,29},{6,30},{7,31},{8,16},{9,... | collective-permute-start | bytes 122888 | tf_op jit(solution)/shard_map/ppermute | solution.py:50
  23.9 0.6 collective-permute-start.6
  24.5 2.3 %collective-permute-start.5 = (bf16[2,16,640]{2,1,0:T(8,128)(2,1)S(1)}, bf16[2,16,640]{2,1,0:T(8,128)(2,1)S(1)}, u32[]{:S(2)}, u32[]{:S(2)}) collective-permute-start(bf16[2,16,640]{2,1,0:T(8,128)(2,1)S(1)} %get-tuple-element.69), channel_id=1, source_target_pairs={{0,8},{1,9},{2,10},{3,11},{4,12},{5,13},{6,14},{7,15},{8,0},{9,1},... | collective-permute-start | bytes 122888 | tf_op jit(solution)/shard_map/ppermute | solution.py:50
  26.8 1.8 %shard_map.176.refs_8_ = bf16[2,352,2048]{2,1,0:T(8,128)(2,1)S(1)} custom-call(bf16[2,64,640]{2,1,0:T(8,128)(2,1)S(1)} %pad_maximum_fusion.refs_0_, bf16[2,2,352,2048]{3,2,1,0:T(8,128)(2,1)} %bitcast.38), custom_call_target="tpu_custom_call" | custom-call | bytes 2883584 | tf_op jit(solution)/shard_map/pallas_call | solution.py:114
  28.7 0.2 collective-permute-done.6
  28.9 0.3 collective-permute-done.5
  29.3 0.6 shard_map.177
  29.9 1.3 %collective-permute-done.8 = bf16[16,2048]{1,0:T(8,128)(2,1)S(1)} collective-permute-done((bf16[16,2048]{1,0:T(8,128)(2,1)S(1)}, bf16[16,2048]{1,0:T(8,128)(2,1)S(1)}, u32[]{:S(2)}, u32[]{:S(2)}) %collective-permute-start.8) | collective-permute-done | bytes 65568 | tf_op jit(solution)/shard_map/ppermute | solution.py:50
  31.2 1.6 %collective-permute-start.9 = (bf16[16,2048]{1,0:T(8,128)(2,1)S(1)}, bf16[16,2048]{1,0:T(8,128)(2,1)S(1)}, u32[]{:S(2)}, u32[]{:S(2)}) collective-permute-start(bf16[16,2048]{1,0:T(8,128)(2,1)S(1)} %fusion.5.refs_0_), channel_id=1, source_target_pairs={{0,2},{1,3},{2,0},{3,1},{4,6},{5,7},{6,4},{7,5},{8,10},{9,11},{10,... | collective-permute-start | bytes 196616 | tf_op jit(solution)/shard_map/ppermute | solution.py:50
  32.9 1.9 %shard_map.178.down_ref = bf16[704,2048]{1,0:T(8,128)(2,1)S(1)} custom-call(bf16[16,2048]{1,0:T(8,128)(2,1)S(1)} %fusion.5.refs_0_, bf16[704,2048]{1,0:T(8,128)(2,1)} %refs_1_.3), custom_call_target="tpu_custom_call" | custom-call | bytes 2883584 | tf_op jit(solution)/shard_map/pallas_call | solution.py:114
  34.7 0.8 %collective-permute-done.9 = bf16[16,2048]{1,0:T(8,128)(2,1)S(1)} collective-permute-done((bf16[16,2048]{1,0:T(8,128)(2,1)S(1)}, bf16[16,2048]{1,0:T(8,128)(2,1)S(1)}, u32[]{:S(2)}, u32[]{:S(2)}) %collective-permute-start.9) | collective-permute-done | bytes 65568 | tf_op jit(solution)/shard_map/ppermute | solution.py:50
  35.7 1.7 %collective-permute-start.10 = (bf16[32,1024]{1,0:T(8,128)(2,1)S(1)}, bf16[32,1024]{1,0:T(8,128)(2,1)S(1)}, u32[]{:S(2)}, u32[]{:S(2)}) collective-permute-start(bf16[32,1024]{1,0:T(8,128)(2,1)S(1)} %pad_maximum_fusion.4), channel_id=1, source_target_pairs={{0,16},{1,25},{2,18},{3,27},{4,20},{5,29},{6,22},{7,31},{8,24},{9,... | collective-permute-start | bytes 196616 | tf_op jit(solution)/shard_map/ppermute | solution.py:67
  37.3 1.3 %collective-permute-start.11 = (bf16[16,1024]{1,0:T(8,128)(2,1)S(1)}, bf16[16,1024]{1,0:T(8,128)(2,1)S(1)}, u32[]{:S(2)}, u32[]{:S(2)}) collective-permute-start(bf16[16,1024]{1,0:T(8,128)(2,1)S(1)} %get-tuple-element.76), channel_id=1, source_target_pairs={{0,8},{1,9},{2,10},{3,11},{4,12},{5,13},{6,14},{7,15},{8,0},{9,1},... | collective-permute-start | bytes 98312 | tf_op jit(solution)/shard_map/ppermute | solution.py:50
  38.6 1.8 %shard_map.179.gate_ref = bf16[704,2048]{1,0:T(8,128)(2,1)S(1)} custom-call(f32[16,2048]{1,0:T(8,128)S(1)} %convert_add_fusion.1.refs_0_.residual_ref, bf16[2,704,2048]{2,1,0:T(8,128)(2,1)} %bitcast.39), custom_call_target="tpu_custom_call" | custom-call | bytes 2883584 | tf_op jit(solution)/shard_map/pallas_call | solution.py:114
  40.5 0.8 %collective-permute-done.11 = bf16[16,1024]{1,0:T(8,128)(2,1)S(1)} collective-permute-done((bf16[16,1024]{1,0:T(8,128)(2,1)S(1)}, bf16[16,1024]{1,0:T(8,128)(2,1)S(1)}, u32[]{:S(2)}, u32[]{:S(2)}) %collective-permute-start.11) | collective-permute-done | bytes 32800 | tf_op jit(solution)/shard_map/ppermute | solution.py:50
  41.4 1.6 %collective-permute-start.12 = (bf16[64,1024]{1,0:T(8,128)(2,1)S(1)}, bf16[64,1024]{1,0:T(8,128)(2,1)S(1)}, u32[]{:S(2)}, u32[]{:S(2)}) collective-permute-start(bf16[64,1024]{1,0:T(8,128)(2,1)S(1)} %pad_maximum_fusion.2.refs_0_), channel_id=1, source_target_pairs={{0,4},{1,5},{2,6},{3,7},{4,0},{5,1},{6,2},{7,3},{8,12},{9,13},{10,... | collective-permute-start | bytes 393224 | tf_op jit(solution)/shard_map/ppermute | solution.py:50
  42.9 3.3 %shard_map.180.refs_6_.shared_ref = f32[16,2048]{1,0:T(8,128)S(1)} custom-call(f32[16,2048]{1,0:T(8,128)S(1)} %convert_add_fusion.1.refs_0_.residual_ref, f32[1,2048]{1,0:T(1,128)S(1)} %bitcast.35, bf16[704,2048]{1,0:T(8,128)(2,1)S(1)} %shard_map.179.gate_ref, bf16[704,2048]{1,0:T(8,128)(2,1)S(1)} %shard_map.178.down_ref, bf16[2,704,2048]{2,1,0:T(8,128)(2,1)} %bitcast.40), custom_call_target="tpu_custom_call" | custom-call | flops 138412032 | bytes 8650752 | tf_op jit(solution)/shard_map/pallas_call | solution.py:114
  46.2 0.4 collective-permute-done.12.refs_1_
  46.8 1.2 %collective-permute-done.14.refs_3_ = bf16[64,1024]{1,0:T(8,128)(2,1)S(1)} collective-permute-done((bf16[64,1024]{1,0:T(8,128)(2,1)S(1)}, bf16[64,1024]{1,0:T(8,128)(2,1)S(1)}, u32[]{:S(2)}, u32[]{:S(2)}) %collective-permute-start.14) | collective-permute-done | bytes 131104 | tf_op jit(solution)/shard_map/ppermute | solution.py:50
  48.0 2.6 %shard_map.181 = (bf16[2,128,512]{2,1,0:T(8,128)(2,1)S(1)}, bf16[2,128,352]{2,1,0:T(8,128)(2,1)S(1)}, bf16[2,352,2048]{2,1,0:T(8,128)(2,1)S(1)}) custom-call(bf16[64,1024]{1,0:T(8,128)(2,1)S(1)} %pad_maximum_fusion.2.refs_0_, bf16[64,1024]{1,0:T(8,128)(2,1)S(1)} %collective-permute-done.12.refs_1_, bf16[64,1024]{1,0:T(8,128)(2,1)S(1)} %collective-permute-done.13.refs_2_, ...), custom_call_target="tpu_custom_call" | custom-call | flops 922746880 | bytes 7208960 | tf_op jit(solution)/shard_map/pallas_call | solution.py:114
  50.6 0.3 collective-permute-start.15
  50.9 0.4 shard_map.182
  51.3 0.9 %collective-permute-done.15 = bf16[2,128,512]{2,1,0:T(8,128)(2,1)S(1)} collective-permute-done((bf16[2,128,512]{2,1,0:T(8,128)(2,1)S(1)}, bf16[2,128,512]{2,1,0:T(8,128)(2,1)S(1)}, u32[]{:S(2)}, u32[]{:S(2)}) %collective-permute-start.15) | collective-permute-done | bytes 262176 | tf_op jit(solution)/shard_map/ppermute | solution.py:50
  52.3 1.6 %collective-permute-start.16 = (bf16[64,512]{1,0:T(8,128)(2,1)S(1)}, bf16[64,512]{1,0:T(8,128)(2,1)S(1)}, u32[]{:S(2)}, u32[]{:S(2)}) collective-permute-start(bf16[64,512]{1,0:T(8,128)(2,1)S(1)} %get-tuple-element.63), channel_id=1, source_target_pairs={{0,4},{1,5},{2,6},{3,7},{4,0},{5,1},{6,2},{7,3},{8,12},{9,13},{10,... | collective-permute-start | bytes 196616 | tf_op jit(solution)/shard_map/ppermute | solution.py:50
  53.9 1.2 %collective-permute-start.18 = (bf16[64,512]{1,0:T(8,128)(2,1)S(1)}, bf16[64,512]{1,0:T(8,128)(2,1)S(1)}, u32[]{:S(2)}, u32[]{:S(2)}) collective-permute-start(bf16[64,512]{1,0:T(8,128)(2,1)S(1)} %get-tuple-element.64), channel_id=1, source_target_pairs={{0,6},{1,7},{2,4},{3,5},{4,2},{5,3},{6,0},{7,1},{8,14},{9,15},{10,... | collective-permute-start | bytes 196616 | tf_op jit(solution)/shard_map/ppermute | solution.py:50
  55.1 0.8 %collective-permute-start.17 = (bf16[64,512]{1,0:T(8,128)(2,1)S(1)}, bf16[64,512]{1,0:T(8,128)(2,1)S(1)}, u32[]{:S(2)}, u32[]{:S(2)}) collective-permute-start(bf16[64,512]{1,0:T(8,128)(2,1)S(1)} %get-tuple-element.65), channel_id=1, source_target_pairs={{0,2},{1,3},{2,0},{3,1},{4,6},{5,7},{6,4},{7,5},{8,10},{9,11},{10,... | collective-permute-start | bytes 196616 | tf_op jit(solution)/shard_map/ppermute | solution.py:50
  55.9 0.8 %collective-permute-done.16 = bf16[64,512]{1,0:T(8,128)(2,1)S(1)} collective-permute-done((bf16[64,512]{1,0:T(8,128)(2,1)S(1)}, bf16[64,512]{1,0:T(8,128)(2,1)S(1)}, u32[]{:S(2)}, u32[]{:S(2)}) %collective-permute-start.16) | collective-permute-done | bytes 65568 | tf_op jit(solution)/shard_map/ppermute | solution.py:50
  56.7 2.9 %collective-permute-done.18 = bf16[64,512]{1,0:T(8,128)(2,1)S(1)} collective-permute-done((bf16[64,512]{1,0:T(8,128)(2,1)S(1)}, bf16[64,512]{1,0:T(8,128)(2,1)S(1)}, u32[]{:S(2)}, u32[]{:S(2)}) %collective-permute-start.18) | collective-permute-done | bytes 65568 | tf_op jit(solution)/shard_map/ppermute | solution.py:50
  59.6 1.2 %collective-permute-start.19 = (bf16[16,512]{1,0:T(8,128)(2,1)S(1)}, bf16[16,512]{1,0:T(8,128)(2,1)S(1)}, u32[]{:S(2)}, u32[]{:S(2)}) collective-permute-start(bf16[16,512]{1,0:T(8,128)(2,1)S(1)} %get-tuple-element.72), channel_id=1, source_target_pairs={{0,8},{1,9},{2,10},{3,11},{4,12},{5,13},{6,14},{7,15},{8,0},{9,1},... | collective-permute-start | bytes 49160 | tf_op jit(solution)/shard_map/ppermute | solution.py:50
  60.8 1.7 %collective-permute-start.21 = (bf16[16,512]{1,0:T(8,128)(2,1)S(1)}, bf16[16,512]{1,0:T(8,128)(2,1)S(1)}, u32[]{:S(2)}, u32[]{:S(2)}) collective-permute-start(bf16[16,512]{1,0:T(8,128)(2,1)S(1)} %get-tuple-element.73), channel_id=1, source_target_pairs={{0,24},{1,25},{2,26},{3,27},{4,28},{5,29},{6,30},{7,31},{8,16},{9,... | collective-permute-start | bytes 49160 | tf_op jit(solution)/shard_map/ppermute | solution.py:50
  62.5 0.6 collective-permute-start.20
  63.2 0.2 collective-permute-done.19
  63.4 2.9 %collective-permute-done.21 = bf16[16,512]{1,0:T(8,128)(2,1)S(1)} collective-permute-done((bf16[16,512]{1,0:T(8,128)(2,1)S(1)}, bf16[16,512]{1,0:T(8,128)(2,1)S(1)}, u32[]{:S(2)}, u32[]{:S(2)}) %collective-permute-start.21) | collective-permute-done | bytes 16416 | tf_op jit(solution)/shard_map/ppermute | solution.py:50
  66.3 0.8 %collective-permute-done.20 = bf16[16,512]{1,0:T(8,128)(2,1)S(1)} collective-permute-done((bf16[16,512]{1,0:T(8,128)(2,1)S(1)}, bf16[16,512]{1,0:T(8,128)(2,1)S(1)}, u32[]{:S(2)}, u32[]{:S(2)}) %collective-permute-start.20) | collective-permute-done | bytes 16416 | tf_op jit(solution)/shard_map/ppermute | solution.py:50
  67.2 0.6 fusion.10
  (50 shorter events, 1.4 us)
Async XLA Ops:
  0.0 7.8 %copy-start = (bf16[2048,2,128]{2,1,0:T(2,128)(2,1)S(1)}, bf16[2048,2,128]{2,1,0:T(2,128)(2,1)}, u32[]{:S(2)}) copy-start(bf16[2048,2,128]{2,1,0:T(2,128)(2,1)} %param.26) | copy-start | bytes 3145732
  0.0 8.2 %copy-start.4 = (s32[64]{0:T(128)S(1)}, s32[64]{0:T(128)}, u32[]{:S(2)}) copy-start(s32[64]{0:T(128)} %param.20) | copy-start | bytes 772
  0.0 8.6 %copy-start.3 = (s32[64]{0:T(128)S(1)}, s32[64]{0:T(128)}, u32[]{:S(2)}) copy-start(s32[64]{0:T(128)} %param.21) | copy-start | bytes 772
  2.1 6.9 %collective-permute-start.2 = (bf16[16,640]{1,0:T(8,128)(2,1)S(1)}, bf16[16,640]{1,0:T(8,128)(2,1)S(1)}, u32[]{:S(2)}, u32[]{:S(2)}) collective-permute-start(bf16[16,640]{1,0:T(8,128)(2,1)S(1)} %get-tuple-element.32.query_ref), channel_id=1, source_target_pairs={{0,24},{1,25},{2,26},{3,27},{4,28},{5,29},{6,30},{7,31},{8,16},{9,... | collective-permute-start | bytes 61448 | tf_op jit(solution)/shard_map/ppermute | solution.py:50
  7.2 4.7 %collective-permute-start.1 = (bf16[16,640]{1,0:T(8,128)(2,1)S(1)}, bf16[16,640]{1,0:T(8,128)(2,1)S(1)}, u32[]{:S(2)}, u32[]{:S(2)}) collective-permute-start(bf16[16,640]{1,0:T(8,128)(2,1)S(1)} %get-tuple-element.32.query_ref), channel_id=1, source_target_pairs={{0,16},{1,17},{2,18},{3,19},{4,20},{5,21},{6,22},{7,23},{8,24},{9,... | collective-permute-start | bytes 61448 | tf_op jit(solution)/shard_map/ppermute | solution.py:50
  7.2 4.7 %collective-permute-start = (bf16[16,640]{1,0:T(8,128)(2,1)S(1)}, bf16[16,640]{1,0:T(8,128)(2,1)S(1)}, u32[]{:S(2)}, u32[]{:S(2)}) collective-permute-start(bf16[16,640]{1,0:T(8,128)(2,1)S(1)} %get-tuple-element.32.query_ref), channel_id=1, source_target_pairs={{0,8},{1,9},{2,10},{3,11},{4,12},{5,13},{6,14},{7,15},{8,0},{9,1},... | collective-permute-start | bytes 61448 | tf_op jit(solution)/shard_map/ppermute | solution.py:50
  11.9 4.5 %collective-permute-start.3 = (bf16[64,640]{1,0:T(8,128)(2,1)S(1)}, bf16[64,640]{1,0:T(8,128)(2,1)S(1)}, u32[]{:S(2)}, u32[]{:S(2)}) collective-permute-start(bf16[64,640]{1,0:T(8,128)(2,1)S(1)} %pad_maximum_fusion.3.refs_0_), channel_id=1, source_target_pairs={{0,4},{1,5},{2,6},{3,7},{4,0},{5,1},{6,2},{7,3},{8,12},{9,13},{10,... | collective-permute-start | bytes 245768 | tf_op jit(solution)/shard_map/ppermute | solution.py:50
  17.8 4.5 %collective-permute-start.4 = (bf16[1,64,640]{2,1,0:T(8,128)(2,1)S(1)}, bf16[1,64,640]{2,1,0:T(8,128)(2,1)S(1)}, u32[]{:S(2)}, u32[]{:S(2)}) collective-permute-start(bf16[1,64,640]{2,1,0:T(8,128)(2,1)S(1)} %get-tuple-element.71), channel_id=1, source_target_pairs={{0,4},{1,5},{2,6},{3,7},{4,0},{5,1},{6,2},{7,3},{8,12},{9,13},{10,... | collective-permute-start | bytes 245768 | tf_op jit(solution)/shard_map/ppermute | solution.py:50
  22.4 6.3 %collective-permute-start.7 = (bf16[2,16,640]{2,1,0:T(8,128)(2,1)S(1)}, bf16[2,16,640]{2,1,0:T(8,128)(2,1)S(1)}, u32[]{:S(2)}, u32[]{:S(2)}) collective-permute-start(bf16[2,16,640]{2,1,0:T(8,128)(2,1)S(1)} %get-tuple-element.67), channel_id=1, source_target_pairs={{0,24},{1,25},{2,26},{3,27},{4,28},{5,29},{6,30},{7,31},{8,16},{9,... | collective-permute-start | bytes 122888 | tf_op jit(solution)/shard_map/ppermute | solution.py:50
  23.9 5.0 %collective-permute-start.6 = (bf16[2,16,640]{2,1,0:T(8,128)(2,1)S(1)}, bf16[2,16,640]{2,1,0:T(8,128)(2,1)S(1)}, u32[]{:S(2)}, u32[]{:S(2)}) collective-permute-start(bf16[2,16,640]{2,1,0:T(8,128)(2,1)S(1)} %get-tuple-element.68), channel_id=1, source_target_pairs={{0,16},{1,17},{2,18},{3,19},{4,20},{5,21},{6,22},{7,23},{8,24},{9,... | collective-permute-start | bytes 122888 | tf_op jit(solution)/shard_map/ppermute | solution.py:50
  24.5 4.7 %collective-permute-start.5 = (bf16[2,16,640]{2,1,0:T(8,128)(2,1)S(1)}, bf16[2,16,640]{2,1,0:T(8,128)(2,1)S(1)}, u32[]{:S(2)}, u32[]{:S(2)}) collective-permute-start(bf16[2,16,640]{2,1,0:T(8,128)(2,1)S(1)} %get-tuple-element.69), channel_id=1, source_target_pairs={{0,8},{1,9},{2,10},{3,11},{4,12},{5,13},{6,14},{7,15},{8,0},{9,1},... | collective-permute-start | bytes 122888 | tf_op jit(solution)/shard_map/ppermute | solution.py:50
  29.9 1.3 %collective-permute-start.8 = (bf16[16,2048]{1,0:T(8,128)(2,1)S(1)}, bf16[16,2048]{1,0:T(8,128)(2,1)S(1)}, u32[]{:S(2)}, u32[]{:S(2)}) collective-permute-start(bf16[16,2048]{1,0:T(8,128)(2,1)S(1)} %get-tuple-element.46), channel_id=1, source_target_pairs={{0,1},{1,0},{2,3},{3,2},{4,5},{5,4},{6,7},{7,6},{8,9},{9,8},{10,11... | collective-permute-start | bytes 196616 | tf_op jit(solution)/shard_map/ppermute | solution.py:50
  31.2 4.3 %collective-permute-start.9 = (bf16[16,2048]{1,0:T(8,128)(2,1)S(1)}, bf16[16,2048]{1,0:T(8,128)(2,1)S(1)}, u32[]{:S(2)}, u32[]{:S(2)}) collective-permute-start(bf16[16,2048]{1,0:T(8,128)(2,1)S(1)} %fusion.5.refs_0_), channel_id=1, source_target_pairs={{0,2},{1,3},{2,0},{3,1},{4,6},{5,7},{6,4},{7,5},{8,10},{9,11},{10,... | collective-permute-start | bytes 196616 | tf_op jit(solution)/shard_map/ppermute | solution.py:50
  32.9 2.7 %copy-start.2 = (bf16[16,2048]{1,0:T(8,128)(2,1)S(1)}, bf16[16,2048]{1,0:T(8,128)(2,1)}, u32[]{:S(2)}) copy-start(bf16[16,2048]{1,0:T(8,128)(2,1)} %hidden_hbm.1) | copy-start | bytes 196612
  35.7 5.7 %collective-permute-start.10 = (bf16[32,1024]{1,0:T(8,128)(2,1)S(1)}, bf16[32,1024]{1,0:T(8,128)(2,1)S(1)}, u32[]{:S(2)}, u32[]{:S(2)}) collective-permute-start(bf16[32,1024]{1,0:T(8,128)(2,1)S(1)} %pad_maximum_fusion.4), channel_id=1, source_target_pairs={{0,16},{1,25},{2,18},{3,27},{4,20},{5,29},{6,22},{7,31},{8,24},{9,... | collective-permute-start | bytes 196616 | tf_op jit(solution)/shard_map/ppermute | solution.py:67
  37.3 4.0 %collective-permute-start.11 = (bf16[16,1024]{1,0:T(8,128)(2,1)S(1)}, bf16[16,1024]{1,0:T(8,128)(2,1)S(1)}, u32[]{:S(2)}, u32[]{:S(2)}) collective-permute-start(bf16[16,1024]{1,0:T(8,128)(2,1)S(1)} %get-tuple-element.76), channel_id=1, source_target_pairs={{0,8},{1,9},{2,10},{3,11},{4,12},{5,13},{6,14},{7,15},{8,0},{9,1},... | collective-permute-start | bytes 98312 | tf_op jit(solution)/shard_map/ppermute | solution.py:50
  38.6 4.3 %copy-start.1 = (f32[2048]{0:T(1024)S(1)}, f32[2048]{0:T(1024)}, u32[]{:S(2)}) copy-start(f32[2048]{0:T(1024)} %param.28) | copy-start | bytes 24580
  41.4 5.3 %collective-permute-start.12 = (bf16[64,1024]{1,0:T(8,128)(2,1)S(1)}, bf16[64,1024]{1,0:T(8,128)(2,1)S(1)}, u32[]{:S(2)}, u32[]{:S(2)}) collective-permute-start(bf16[64,1024]{1,0:T(8,128)(2,1)S(1)} %pad_maximum_fusion.2.refs_0_), channel_id=1, source_target_pairs={{0,4},{1,5},{2,6},{3,7},{4,0},{5,1},{6,2},{7,3},{8,12},{9,13},{10,... | collective-permute-start | bytes 393224 | tf_op jit(solution)/shard_map/ppermute | solution.py:50
  42.9 3.9 %collective-permute-start.13 = (bf16[64,1024]{1,0:T(8,128)(2,1)S(1)}, bf16[64,1024]{1,0:T(8,128)(2,1)S(1)}, u32[]{:S(2)}, u32[]{:S(2)}) collective-permute-start(bf16[64,1024]{1,0:T(8,128)(2,1)S(1)} %pad_maximum_fusion.2.refs_0_), channel_id=1, source_target_pairs={{0,1},{1,0},{2,3},{3,2},{4,5},{5,4},{6,7},{7,6},{8,9},{9,8},{10,11... | collective-permute-start | bytes 393224 | tf_op jit(solution)/shard_map/ppermute | solution.py:50
  46.6 1.3 %collective-permute-start.14 = (bf16[64,1024]{1,0:T(8,128)(2,1)S(1)}, bf16[64,1024]{1,0:T(8,128)(2,1)S(1)}, u32[]{:S(2)}, u32[]{:S(2)}) collective-permute-start(bf16[64,1024]{1,0:T(8,128)(2,1)S(1)} %collective-permute-done.12.refs_1_), channel_id=1, source_target_pairs={{0,1},{1,0},{2,3},{3,2},{4,5},{5,4},{6,7},{7,6},{8,9},{9,8},{10,11... | collective-permute-start | bytes 393224 | tf_op jit(solution)/shard_map/ppermute | solution.py:50
  50.6 1.6 %collective-permute-start.15 = (bf16[2,128,512]{2,1,0:T(8,128)(2,1)S(1)}, bf16[2,128,512]{2,1,0:T(8,128)(2,1)S(1)}, u32[]{:S(2)}, u32[]{:S(2)}) collective-permute-start(bf16[2,128,512]{2,1,0:T(8,128)(2,1)S(1)} %get-tuple-element.58), channel_id=1, source_target_pairs={{0,1},{1,0},{2,3},{3,2},{4,5},{5,4},{6,7},{7,6},{8,9},{9,8},{10,11... | collective-permute-start | bytes 786440 | tf_op jit(solution)/shard_map/ppermute | solution.py:50
  52.3 4.3 %collective-permute-start.16 = (bf16[64,512]{1,0:T(8,128)(2,1)S(1)}, bf16[64,512]{1,0:T(8,128)(2,1)S(1)}, u32[]{:S(2)}, u32[]{:S(2)}) collective-permute-start(bf16[64,512]{1,0:T(8,128)(2,1)S(1)} %get-tuple-element.63), channel_id=1, source_target_pairs={{0,4},{1,5},{2,6},{3,7},{4,0},{5,1},{6,2},{7,3},{8,12},{9,13},{10,... | collective-permute-start | bytes 196616 | tf_op jit(solution)/shard_map/ppermute | solution.py:50
  53.9 5.6 %collective-permute-start.18 = (bf16[64,512]{1,0:T(8,128)(2,1)S(1)}, bf16[64,512]{1,0:T(8,128)(2,1)S(1)}, u32[]{:S(2)}, u32[]{:S(2)}) collective-permute-start(bf16[64,512]{1,0:T(8,128)(2,1)S(1)} %get-tuple-element.64), channel_id=1, source_target_pairs={{0,6},{1,7},{2,4},{3,5},{4,2},{5,3},{6,0},{7,1},{8,14},{9,15},{10,... | collective-permute-start | bytes 196616 | tf_op jit(solution)/shard_map/ppermute | solution.py:50
  55.1 4.5 %collective-permute-start.17 = (bf16[64,512]{1,0:T(8,128)(2,1)S(1)}, bf16[64,512]{1,0:T(8,128)(2,1)S(1)}, u32[]{:S(2)}, u32[]{:S(2)}) collective-permute-start(bf16[64,512]{1,0:T(8,128)(2,1)S(1)} %get-tuple-element.65), channel_id=1, source_target_pairs={{0,2},{1,3},{2,0},{3,1},{4,6},{5,7},{6,4},{7,5},{8,10},{9,11},{10,... | collective-permute-start | bytes 196616 | tf_op jit(solution)/shard_map/ppermute | solution.py:50
  59.6 3.8 %collective-permute-start.19 = (bf16[16,512]{1,0:T(8,128)(2,1)S(1)}, bf16[16,512]{1,0:T(8,128)(2,1)S(1)}, u32[]{:S(2)}, u32[]{:S(2)}) collective-permute-start(bf16[16,512]{1,0:T(8,128)(2,1)S(1)} %get-tuple-element.72), channel_id=1, source_target_pairs={{0,8},{1,9},{2,10},{3,11},{4,12},{5,13},{6,14},{7,15},{8,0},{9,1},... | collective-permute-start | bytes 49160 | tf_op jit(solution)/shard_map/ppermute | solution.py:50
  60.8 5.5 %collective-permute-start.21 = (bf16[16,512]{1,0:T(8,128)(2,1)S(1)}, bf16[16,512]{1,0:T(8,128)(2,1)S(1)}, u32[]{:S(2)}, u32[]{:S(2)}) collective-permute-start(bf16[16,512]{1,0:T(8,128)(2,1)S(1)} %get-tuple-element.73), channel_id=1, source_target_pairs={{0,24},{1,25},{2,26},{3,27},{4,28},{5,29},{6,30},{7,31},{8,16},{9,... | collective-permute-start | bytes 49160 | tf_op jit(solution)/shard_map/ppermute | solution.py:50
  62.5 4.6 %collective-permute-start.20 = (bf16[16,512]{1,0:T(8,128)(2,1)S(1)}, bf16[16,512]{1,0:T(8,128)(2,1)S(1)}, u32[]{:S(2)}, u32[]{:S(2)}) collective-permute-start(bf16[16,512]{1,0:T(8,128)(2,1)S(1)} %get-tuple-element.74), channel_id=1, source_target_pairs={{0,16},{1,17},{2,18},{3,19},{4,20},{5,21},{6,22},{7,23},{8,24},{9,... | collective-permute-start | bytes 49160 | tf_op jit(solution)/shard_map/ppermute | solution.py:50

commit v3 on v2

--- a/solution.py
+++ b/solution.py
@@ -103,7 +103,7 @@
     for shift, size in plan:
         part = blocks.shape[0] // size
         total = blocks[:part]
-        for i in range(1, size):
+        for i in reversed(range(1, size)):
             sent = blocks[i * part : (i + 1) * part].astype(BF)
             total = total + swap(sent, i << shift).astype(F32)
         blocks = total

time: 68.1 us -> 67.9 us (level)
  waiting for transfers between devices: 17.8 us -> 16.7 us
  starting transfers between devices: 27.1 us -> 28 us
    ppermute x21, waiting for transfers between devices: 17.8 us -> 16.7 us  [swap(): lax.ppermute(value, REQ + HEAD, [(i, i ^ step) for i in range(count)])]
    ppermute x21, starting transfers between devices: 25.4 us -> 26.3 us  [swap(): lax.ppermute(value, REQ + HEAD, [(i, i ^ step) for i in range(count)])]
where the time goes in v3:
time: 67.9 us; the launch traced here: 67.6 us
  starting transfers between devices  28 us (41%)
  Pallas kernels  20.6 us (30%)
  waiting for transfers between devices  16.7 us (25%)
  other arithmetic  1.24 us (2%)
    ppermute x21, starting transfers between devices, swap(): lax.ppermute(value, REQ + HEAD, [(i, i ^ step) for i in range(count)])  26.3 us
    pallas_call x11, Pallas kernels, call(): pl.pallas_call(kernel, out_shape=out_shape, in_specs=specs or [VMEM] * le...  20.6 us
    ppermute x21, waiting for transfers between devices, swap(): lax.ppermute(value, REQ + HEAD, [(i, i ^ step) for i in range(count)])  16.7 us
    ppermute x1, starting transfers between devices, trade(): lax.ppermute(whole, REQ + HEAD, [(i, i ^ steps[i % 2]) for i in range(cou...  1.66 us
  transfers between devices with their start and end apart: 22, of which 17 were waited for; matrix products, arithmetic and copies ran while one was open for 1% of the time, Pallas kernels for 21%

profile of v3, /device:TPU:0, one launch (start us, length us, event | category | flops | bytes accessed | tf_op | source)
XLA Modules:
  0.0 67.6 jit_solution(6268975032834139243)
XLA Ops:
  0.0 2.0 %shard_map.172 = (bf16[16,640]{1,0:T(8,128)(2,1)S(1)}, f32[16,384]{1,0:T(8,128)S(1)}, bf16[16,2048]{1,0:T(8,128)(2,1)S(1)}) custom-call(s32[1,16]{1,0:T(1,128)} %bitcast.46, f32[1,128]{1,0:T(1,128)} %constant.61.clone.freq_hbm, s32[6,16]{1,0:T(8,128)} %bitcast.44, f32[6,16]{1,0:T(8,128)} %bitcast.45, bf16[16,2048]{1,0:T(8,128)(2,1)} %hidden_hbm.1, ...), custom_call_target="tpu_custom_call" | custom-call | flops 33554432 | bytes 2097152 | tf_op jit(solution)/shard_map/pallas_call | solution.py:114
  2.1 5.1 %collective-permute-start.2 = (bf16[16,640]{1,0:T(8,128)(2,1)S(1)}, bf16[16,640]{1,0:T(8,128)(2,1)S(1)}, u32[]{:S(2)}, u32[]{:S(2)}) collective-permute-start(bf16[16,640]{1,0:T(8,128)(2,1)S(1)} %get-tuple-element.32.query_ref), channel_id=1, source_target_pairs={{0,24},{1,25},{2,26},{3,27},{4,28},{5,29},{6,30},{7,31},{8,16},{9,... | collective-permute-start | bytes 61448 | tf_op jit(solution)/shard_map/ppermute | solution.py:50
  7.2 0.6 collective-permute-start
  7.8 0.2 fusion
  8.7 0.2 collective-permute-done.2
  8.9 2.9 %collective-permute-done.1 = bf16[16,640]{1,0:T(8,128)(2,1)S(1)} collective-permute-done((bf16[16,640]{1,0:T(8,128)(2,1)S(1)}, bf16[16,640]{1,0:T(8,128)(2,1)S(1)}, u32[]{:S(2)}, u32[]{:S(2)}) %collective-permute-start.1) | collective-permute-done | bytes 20512 | tf_op jit(solution)/shard_map/ppermute | solution.py:50
  11.9 1.6 %collective-permute-start.3 = (bf16[64,640]{1,0:T(8,128)(2,1)S(1)}, bf16[64,640]{1,0:T(8,128)(2,1)S(1)}, u32[]{:S(2)}, u32[]{:S(2)}) collective-permute-start(bf16[64,640]{1,0:T(8,128)(2,1)S(1)} %pad_maximum_fusion.3.refs_0_), channel_id=1, source_target_pairs={{0,4},{1,5},{2,6},{3,7},{4,0},{5,1},{6,2},{7,3},{8,12},{9,13},{10,... | collective-permute-start | bytes 245768 | tf_op jit(solution)/shard_map/ppermute | solution.py:50
  13.5 2.2 %shard_map.173 = (bf16[64,128,128]{2,1,0:T(8,128)(2,1)S(1)}, bf16[64,128,128]{2,1,0:T(8,128)(2,1)S(1)}) custom-call(bf16[64,640]{1,0:T(8,128)(2,1)S(1)} %pad_maximum_fusion.3.refs_0_, bf16[64,128,128]{2,1,0:T(8,128)(2,1)} %bitcast.41, bf16[64,128,128]{2,1,0:T(8,128)(2,1)} %bitcast.42), custom_call_target="tpu_custom_call" | custom-call | bytes 4194304 | tf_op jit(solution)/shard_map/pallas_call | solution.py:114
  15.7 0.7 collective-permute-done.3
  16.4 1.4 %shard_map.174.refs_0_ = bf16[128,640]{1,0:T(8,128)(2,1)S(1)} custom-call(bf16[128,640]{1,0:T(8,128)(2,1)S(1)} %constant_dynamic-update-slice_fusion.query_ref, s32[256,1]{1,0:T(8,128)S(1)} %add.114.column_ref, s32[1,256]{1,0:T(1,128)S(1)} %add.100.row_ref, s32[256,1]{1,0:T(8,128)S(1)} %broadcast_in_dim_reshape.6.fill_ref, ...), custom_call_target="tpu_custom_call" | custom-call | flops 67108864 | bytes 4194304 | tf_op jit(solution)/shard_map/pallas_call | solution.py:114
  17.8 1.6 %collective-permute-start.4 = (bf16[1,64,640]{2,1,0:T(8,128)(2,1)S(1)}, bf16[1,64,640]{2,1,0:T(8,128)(2,1)S(1)}, u32[]{:S(2)}, u32[]{:S(2)}) collective-permute-start(bf16[1,64,640]{2,1,0:T(8,128)(2,1)S(1)} %get-tuple-element.71), channel_id=1, source_target_pairs={{0,4},{1,5},{2,6},{3,7},{4,0},{5,1},{6,2},{7,3},{8,12},{9,13},{10,... | collective-permute-start | bytes 245768 | tf_op jit(solution)/shard_map/ppermute | solution.py:50
  19.4 2.5 %shard_map.175 = (bf16[512,2048]{1,0:T(8,128)(2,1)S(1)}, bf16[2,352,2048]{2,1,0:T(8,128)(2,1)S(1)}) custom-call(bf16[128,640]{1,0:T(8,128)(2,1)S(1)} %shard_map.174.refs_0_, bf16[512,2048]{1,0:T(8,128)(2,1)} %refs_1_.2, bf16[2,2,352,2048]{3,2,1,0:T(8,128)(2,1)} %bitcast.37), custom_call_target="tpu_custom_call" | custom-call | bytes 4980736 | tf_op jit(solution)/shard_map/pallas_call | solution.py:114
  21.9 0.5 collective-permute-done.4
  22.4 1.5 %collective-permute-start.7 = (bf16[2,16,640]{2,1,0:T(8,128)(2,1)S(1)}, bf16[2,16,640]{2,1,0:T(8,128)(2,1)S(1)}, u32[]{:S(2)}, u32[]{:S(2)}) collective-permute-start(bf16[2,16,640]{2,1,0:T(8,128)(2,1)S(1)} %get-tuple-element.67), channel_id=1, source_target_pairs={{0,24},{1,25},{2,26},{3,27},{4,28},{5,29},{6,30},{7,31},{8,16},{9,... | collective-permute-start | bytes 122888 | tf_op jit(solution)/shard_map/ppermute | solution.py:50
  23.9 0.6 collective-permute-start.6
  24.5 2.3 %collective-permute-start.5 = (bf16[2,16,640]{2,1,0:T(8,128)(2,1)S(1)}, bf16[2,16,640]{2,1,0:T(8,128)(2,1)S(1)}, u32[]{:S(2)}, u32[]{:S(2)}) collective-permute-start(bf16[2,16,640]{2,1,0:T(8,128)(2,1)S(1)} %get-tuple-element.69), channel_id=1, source_target_pairs={{0,8},{1,9},{2,10},{3,11},{4,12},{5,13},{6,14},{7,15},{8,0},{9,1},... | collective-permute-start | bytes 122888 | tf_op jit(solution)/shard_map/ppermute | solution.py:50
  26.8 1.8 %shard_map.176.refs_8_ = bf16[2,352,2048]{2,1,0:T(8,128)(2,1)S(1)} custom-call(bf16[2,64,640]{2,1,0:T(8,128)(2,1)S(1)} %pad_maximum_fusion.refs_0_, bf16[2,2,352,2048]{3,2,1,0:T(8,128)(2,1)} %bitcast.38), custom_call_target="tpu_custom_call" | custom-call | bytes 2883584 | tf_op jit(solution)/shard_map/pallas_call | solution.py:114
  28.7 0.2 collective-permute-done.6
  28.9 0.3 collective-permute-done.5
  29.3 0.6 shard_map.177
  29.9 1.3 %collective-permute-done.8 = bf16[16,2048]{1,0:T(8,128)(2,1)S(1)} collective-permute-done((bf16[16,2048]{1,0:T(8,128)(2,1)S(1)}, bf16[16,2048]{1,0:T(8,128)(2,1)S(1)}, u32[]{:S(2)}, u32[]{:S(2)}) %collective-permute-start.8) | collective-permute-done | bytes 65568 | tf_op jit(solution)/shard_map/ppermute | solution.py:50
  31.2 1.6 %collective-permute-start.9 = (bf16[16,2048]{1,0:T(8,128)(2,1)S(1)}, bf16[16,2048]{1,0:T(8,128)(2,1)S(1)}, u32[]{:S(2)}, u32[]{:S(2)}) collective-permute-start(bf16[16,2048]{1,0:T(8,128)(2,1)S(1)} %fusion.5.refs_0_), channel_id=1, source_target_pairs={{0,2},{1,3},{2,0},{3,1},{4,6},{5,7},{6,4},{7,5},{8,10},{9,11},{10,... | collective-permute-start | bytes 196616 | tf_op jit(solution)/shard_map/ppermute | solution.py:50
  32.9 1.9 %shard_map.178.down_ref = bf16[704,2048]{1,0:T(8,128)(2,1)S(1)} custom-call(bf16[16,2048]{1,0:T(8,128)(2,1)S(1)} %fusion.5.refs_0_, bf16[704,2048]{1,0:T(8,128)(2,1)} %refs_1_.3), custom_call_target="tpu_custom_call" | custom-call | bytes 2883584 | tf_op jit(solution)/shard_map/pallas_call | solution.py:114
  34.7 0.8 %collective-permute-done.9 = bf16[16,2048]{1,0:T(8,128)(2,1)S(1)} collective-permute-done((bf16[16,2048]{1,0:T(8,128)(2,1)S(1)}, bf16[16,2048]{1,0:T(8,128)(2,1)S(1)}, u32[]{:S(2)}, u32[]{:S(2)}) %collective-permute-start.9) | collective-permute-done | bytes 65568 | tf_op jit(solution)/shard_map/ppermute | solution.py:50
  35.7 1.7 %collective-permute-start.10 = (bf16[32,1024]{1,0:T(8,128)(2,1)S(1)}, bf16[32,1024]{1,0:T(8,128)(2,1)S(1)}, u32[]{:S(2)}, u32[]{:S(2)}) collective-permute-start(bf16[32,1024]{1,0:T(8,128)(2,1)S(1)} %pad_maximum_fusion.4), channel_id=1, source_target_pairs={{0,16},{1,25},{2,18},{3,27},{4,20},{5,29},{6,22},{7,31},{8,24},{9,... | collective-permute-start | bytes 196616 | tf_op jit(solution)/shard_map/ppermute | solution.py:67
  37.3 1.3 %collective-permute-start.11 = (bf16[16,1024]{1,0:T(8,128)(2,1)S(1)}, bf16[16,1024]{1,0:T(8,128)(2,1)S(1)}, u32[]{:S(2)}, u32[]{:S(2)}) collective-permute-start(bf16[16,1024]{1,0:T(8,128)(2,1)S(1)} %get-tuple-element.76), channel_id=1, source_target_pairs={{0,8},{1,9},{2,10},{3,11},{4,12},{5,13},{6,14},{7,15},{8,0},{9,1},... | collective-permute-start | bytes 98312 | tf_op jit(solution)/shard_map/ppermute | solution.py:50
  38.6 1.8 %shard_map.179.gate_ref = bf16[704,2048]{1,0:T(8,128)(2,1)S(1)} custom-call(f32[16,2048]{1,0:T(8,128)S(1)} %convert_add_fusion.1.refs_0_.residual_ref, bf16[2,704,2048]{2,1,0:T(8,128)(2,1)} %bitcast.39), custom_call_target="tpu_custom_call" | custom-call | bytes 2883584 | tf_op jit(solution)/shard_map/pallas_call | solution.py:114
  40.5 0.8 %collective-permute-done.11 = bf16[16,1024]{1,0:T(8,128)(2,1)S(1)} collective-permute-done((bf16[16,1024]{1,0:T(8,128)(2,1)S(1)}, bf16[16,1024]{1,0:T(8,128)(2,1)S(1)}, u32[]{:S(2)}, u32[]{:S(2)}) %collective-permute-start.11) | collective-permute-done | bytes 32800 | tf_op jit(solution)/shard_map/ppermute | solution.py:50
  41.4 1.6 %collective-permute-start.12 = (bf16[64,1024]{1,0:T(8,128)(2,1)S(1)}, bf16[64,1024]{1,0:T(8,128)(2,1)S(1)}, u32[]{:S(2)}, u32[]{:S(2)}) collective-permute-start(bf16[64,1024]{1,0:T(8,128)(2,1)S(1)} %pad_maximum_fusion.2.refs_0_), channel_id=1, source_target_pairs={{0,4},{1,5},{2,6},{3,7},{4,0},{5,1},{6,2},{7,3},{8,12},{9,13},{10,... | collective-permute-start | bytes 393224 | tf_op jit(solution)/shard_map/ppermute | solution.py:50
  42.9 3.3 %shard_map.180.refs_6_.shared_ref = f32[16,2048]{1,0:T(8,128)S(1)} custom-call(f32[16,2048]{1,0:T(8,128)S(1)} %convert_add_fusion.1.refs_0_.residual_ref, f32[1,2048]{1,0:T(1,128)S(1)} %bitcast.35, bf16[704,2048]{1,0:T(8,128)(2,1)S(1)} %shard_map.179.gate_ref, bf16[704,2048]{1,0:T(8,128)(2,1)S(1)} %shard_map.178.down_ref, bf16[2,704,2048]{2,1,0:T(8,128)(2,1)} %bitcast.40), custom_call_target="tpu_custom_call" | custom-call | flops 138412032 | bytes 8650752 | tf_op jit(solution)/shard_map/pallas_call | solution.py:114
  46.2 0.4 collective-permute-done.12.refs_1_
  46.6 0.2 collective-permute-start.14
  46.8 1.2 %collective-permute-done.14.refs_3_ = bf16[64,1024]{1,0:T(8,128)(2,1)S(1)} collective-permute-done((bf16[64,1024]{1,0:T(8,128)(2,1)S(1)}, bf16[64,1024]{1,0:T(8,128)(2,1)S(1)}, u32[]{:S(2)}, u32[]{:S(2)}) %collective-permute-start.14) | collective-permute-done | bytes 131104 | tf_op jit(solution)/shard_map/ppermute | solution.py:50
  48.0 2.6 %shard_map.181 = (bf16[2,128,512]{2,1,0:T(8,128)(2,1)S(1)}, bf16[2,128,352]{2,1,0:T(8,128)(2,1)S(1)}, bf16[2,352,2048]{2,1,0:T(8,128)(2,1)S(1)}) custom-call(bf16[64,1024]{1,0:T(8,128)(2,1)S(1)} %pad_maximum_fusion.2.refs_0_, bf16[64,1024]{1,0:T(8,128)(2,1)S(1)} %collective-permute-done.12.refs_1_, bf16[64,1024]{1,0:T(8,128)(2,1)S(1)} %collective-permute-done.13.refs_2_, ...), custom_call_target="tpu_custom_call" | custom-call | flops 922746880 | bytes 7208960 | tf_op jit(solution)/shard_map/pallas_call | solution.py:114
  50.6 0.3 collective-permute-start.15
  50.9 0.4 shard_map.182
  51.3 0.9 %collective-permute-done.15 = bf16[2,128,512]{2,1,0:T(8,128)(2,1)S(1)} collective-permute-done((bf16[2,128,512]{2,1,0:T(8,128)(2,1)S(1)}, bf16[2,128,512]{2,1,0:T(8,128)(2,1)S(1)}, u32[]{:S(2)}, u32[]{:S(2)}) %collective-permute-start.15) | collective-permute-done | bytes 262176 | tf_op jit(solution)/shard_map/ppermute | solution.py:50
  52.3 1.6 %collective-permute-start.16 = (bf16[64,512]{1,0:T(8,128)(2,1)S(1)}, bf16[64,512]{1,0:T(8,128)(2,1)S(1)}, u32[]{:S(2)}, u32[]{:S(2)}) collective-permute-start(bf16[64,512]{1,0:T(8,128)(2,1)S(1)} %get-tuple-element.63), channel_id=1, source_target_pairs={{0,4},{1,5},{2,6},{3,7},{4,0},{5,1},{6,2},{7,3},{8,12},{9,13},{10,... | collective-permute-start | bytes 196616 | tf_op jit(solution)/shard_map/ppermute | solution.py:50
  53.9 1.2 %collective-permute-start.18 = (bf16[64,512]{1,0:T(8,128)(2,1)S(1)}, bf16[64,512]{1,0:T(8,128)(2,1)S(1)}, u32[]{:S(2)}, u32[]{:S(2)}) collective-permute-start(bf16[64,512]{1,0:T(8,128)(2,1)S(1)} %get-tuple-element.64), channel_id=1, source_target_pairs={{0,6},{1,7},{2,4},{3,5},{4,2},{5,3},{6,0},{7,1},{8,14},{9,15},{10,... | collective-permute-start | bytes 196616 | tf_op jit(solution)/shard_map/ppermute | solution.py:50
  55.1 0.8 %collective-permute-start.17 = (bf16[64,512]{1,0:T(8,128)(2,1)S(1)}, bf16[64,512]{1,0:T(8,128)(2,1)S(1)}, u32[]{:S(2)}, u32[]{:S(2)}) collective-permute-start(bf16[64,512]{1,0:T(8,128)(2,1)S(1)} %get-tuple-element.65), channel_id=1, source_target_pairs={{0,2},{1,3},{2,0},{3,1},{4,6},{5,7},{6,4},{7,5},{8,10},{9,11},{10,... | collective-permute-start | bytes 196616 | tf_op jit(solution)/shard_map/ppermute | solution.py:50
  55.9 0.8 %collective-permute-done.16 = bf16[64,512]{1,0:T(8,128)(2,1)S(1)} collective-permute-done((bf16[64,512]{1,0:T(8,128)(2,1)S(1)}, bf16[64,512]{1,0:T(8,128)(2,1)S(1)}, u32[]{:S(2)}, u32[]{:S(2)}) %collective-permute-start.16) | collective-permute-done | bytes 65568 | tf_op jit(solution)/shard_map/ppermute | solution.py:50
  56.7 2.9 %collective-permute-done.18 = bf16[64,512]{1,0:T(8,128)(2,1)S(1)} collective-permute-done((bf16[64,512]{1,0:T(8,128)(2,1)S(1)}, bf16[64,512]{1,0:T(8,128)(2,1)S(1)}, u32[]{:S(2)}, u32[]{:S(2)}) %collective-permute-start.18) | collective-permute-done | bytes 65568 | tf_op jit(solution)/shard_map/ppermute | solution.py:50
  59.6 2.7 %collective-permute-start.19 = (bf16[16,512]{1,0:T(8,128)(2,1)S(1)}, bf16[16,512]{1,0:T(8,128)(2,1)S(1)}, u32[]{:S(2)}, u32[]{:S(2)}) collective-permute-start(bf16[16,512]{1,0:T(8,128)(2,1)S(1)} %get-tuple-element.72), channel_id=1, source_target_pairs={{0,24},{1,25},{2,26},{3,27},{4,28},{5,29},{6,30},{7,31},{8,16},{9,... | collective-permute-start | bytes 49160 | tf_op jit(solution)/shard_map/ppermute | solution.py:50
  62.3 1.8 %collective-permute-start.20 = (bf16[16,512]{1,0:T(8,128)(2,1)S(1)}, bf16[16,512]{1,0:T(8,128)(2,1)S(1)}, u32[]{:S(2)}, u32[]{:S(2)}) collective-permute-start(bf16[16,512]{1,0:T(8,128)(2,1)S(1)} %get-tuple-element.74), channel_id=1, source_target_pairs={{0,16},{1,17},{2,18},{3,19},{4,20},{5,21},{6,22},{7,23},{8,24},{9,... | collective-permute-start | bytes 49160 | tf_op jit(solution)/shard_map/ppermute | solution.py:50
  64.1 1.1 %collective-permute-done.19 = bf16[16,512]{1,0:T(8,128)(2,1)S(1)} collective-permute-done((bf16[16,512]{1,0:T(8,128)(2,1)S(1)}, bf16[16,512]{1,0:T(8,128)(2,1)S(1)}, u32[]{:S(2)}, u32[]{:S(2)}) %collective-permute-start.19) | collective-permute-done | bytes 16416 | tf_op jit(solution)/shard_map/ppermute | solution.py:50
  65.2 0.8 %collective-permute-done.21 = bf16[16,512]{1,0:T(8,128)(2,1)S(1)} collective-permute-done((bf16[16,512]{1,0:T(8,128)(2,1)S(1)}, bf16[16,512]{1,0:T(8,128)(2,1)S(1)}, u32[]{:S(2)}, u32[]{:S(2)}) %collective-permute-start.21) | collective-permute-done | bytes 16416 | tf_op jit(solution)/shard_map/ppermute | solution.py:50
  66.0 0.9 %collective-permute-done.20 = bf16[16,512]{1,0:T(8,128)(2,1)S(1)} collective-permute-done((bf16[16,512]{1,0:T(8,128)(2,1)S(1)}, bf16[16,512]{1,0:T(8,128)(2,1)S(1)}, u32[]{:S(2)}, u32[]{:S(2)}) %collective-permute-start.20) | collective-permute-done | bytes 16416 | tf_op jit(solution)/shard_map/ppermute | solution.py:50
  66.9 0.6 fusion.10
  (50 shorter events, 1.2 us)
Async XLA Ops:
  0.0 7.8 %copy-start = (bf16[2048,2,128]{2,1,0:T(2,128)(2,1)S(1)}, bf16[2048,2,128]{2,1,0:T(2,128)(2,1)}, u32[]{:S(2)}) copy-start(bf16[2048,2,128]{2,1,0:T(2,128)(2,1)} %param.26) | copy-start | bytes 3145732
  0.0 8.2 %copy-start.4 = (s32[64]{0:T(128)S(1)}, s32[64]{0:T(128)}, u32[]{:S(2)}) copy-start(s32[64]{0:T(128)} %param.20) | copy-start | bytes 772
  0.0 8.6 %copy-start.3 = (s32[64]{0:T(128)S(1)}, s32[64]{0:T(128)}, u32[]{:S(2)}) copy-start(s32[64]{0:T(128)} %param.21) | copy-start | bytes 772
  2.1 6.9 %collective-permute-start.2 = (bf16[16,640]{1,0:T(8,128)(2,1)S(1)}, bf16[16,640]{1,0:T(8,128)(2,1)S(1)}, u32[]{:S(2)}, u32[]{:S(2)}) collective-permute-start(bf16[16,640]{1,0:T(8,128)(2,1)S(1)} %get-tuple-element.32.query_ref), channel_id=1, source_target_pairs={{0,24},{1,25},{2,26},{3,27},{4,28},{5,29},{6,30},{7,31},{8,16},{9,... | collective-permute-start | bytes 61448 | tf_op jit(solution)/shard_map/ppermute | solution.py:50
  7.2 4.7 %collective-permute-start.1 = (bf16[16,640]{1,0:T(8,128)(2,1)S(1)}, bf16[16,640]{1,0:T(8,128)(2,1)S(1)}, u32[]{:S(2)}, u32[]{:S(2)}) collective-permute-start(bf16[16,640]{1,0:T(8,128)(2,1)S(1)} %get-tuple-element.32.query_ref), channel_id=1, source_target_pairs={{0,16},{1,17},{2,18},{3,19},{4,20},{5,21},{6,22},{7,23},{8,24},{9,... | collective-permute-start | bytes 61448 | tf_op jit(solution)/shard_map/ppermute | solution.py:50
  7.2 4.7 %collective-permute-start = (bf16[16,640]{1,0:T(8,128)(2,1)S(1)}, bf16[16,640]{1,0:T(8,128)(2,1)S(1)}, u32[]{:S(2)}, u32[]{:S(2)}) collective-permute-start(bf16[16,640]{1,0:T(8,128)(2,1)S(1)} %get-tuple-element.32.query_ref), channel_id=1, source_target_pairs={{0,8},{1,9},{2,10},{3,11},{4,12},{5,13},{6,14},{7,15},{8,0},{9,1},... | collective-permute-start | bytes 61448 | tf_op jit(solution)/shard_map/ppermute | solution.py:50
  11.9 4.5 %collective-permute-start.3 = (bf16[64,640]{1,0:T(8,128)(2,1)S(1)}, bf16[64,640]{1,0:T(8,128)(2,1)S(1)}, u32[]{:S(2)}, u32[]{:S(2)}) collective-permute-start(bf16[64,640]{1,0:T(8,128)(2,1)S(1)} %pad_maximum_fusion.3.refs_0_), channel_id=1, source_target_pairs={{0,4},{1,5},{2,6},{3,7},{4,0},{5,1},{6,2},{7,3},{8,12},{9,13},{10,... | collective-permute-start | bytes 245768 | tf_op jit(solution)/shard_map/ppermute | solution.py:50
  17.8 4.5 %collective-permute-start.4 = (bf16[1,64,640]{2,1,0:T(8,128)(2,1)S(1)}, bf16[1,64,640]{2,1,0:T(8,128)(2,1)S(1)}, u32[]{:S(2)}, u32[]{:S(2)}) collective-permute-start(bf16[1,64,640]{2,1,0:T(8,128)(2,1)S(1)} %get-tuple-element.71), channel_id=1, source_target_pairs={{0,4},{1,5},{2,6},{3,7},{4,0},{5,1},{6,2},{7,3},{8,12},{9,13},{10,... | collective-permute-start | bytes 245768 | tf_op jit(solution)/shard_map/ppermute | solution.py:50
  22.4 6.3 %collective-permute-start.7 = (bf16[2,16,640]{2,1,0:T(8,128)(2,1)S(1)}, bf16[2,16,640]{2,1,0:T(8,128)(2,1)S(1)}, u32[]{:S(2)}, u32[]{:S(2)}) collective-permute-start(bf16[2,16,640]{2,1,0:T(8,128)(2,1)S(1)} %get-tuple-element.67), channel_id=1, source_target_pairs={{0,24},{1,25},{2,26},{3,27},{4,28},{5,29},{6,30},{7,31},{8,16},{9,... | collective-permute-start | bytes 122888 | tf_op jit(solution)/shard_map/ppermute | solution.py:50
  23.9 5.0 %collective-permute-start.6 = (bf16[2,16,640]{2,1,0:T(8,128)(2,1)S(1)}, bf16[2,16,640]{2,1,0:T(8,128)(2,1)S(1)}, u32[]{:S(2)}, u32[]{:S(2)}) collective-permute-start(bf16[2,16,640]{2,1,0:T(8,128)(2,1)S(1)} %get-tuple-element.68), channel_id=1, source_target_pairs={{0,16},{1,17},{2,18},{3,19},{4,20},{5,21},{6,22},{7,23},{8,24},{9,... | collective-permute-start | bytes 122888 | tf_op jit(solution)/shard_map/ppermute | solution.py:50
  24.5 4.7 %collective-permute-start.5 = (bf16[2,16,640]{2,1,0:T(8,128)(2,1)S(1)}, bf16[2,16,640]{2,1,0:T(8,128)(2,1)S(1)}, u32[]{:S(2)}, u32[]{:S(2)}) collective-permute-start(bf16[2,16,640]{2,1,0:T(8,128)(2,1)S(1)} %get-tuple-element.69), channel_id=1, source_target_pairs={{0,8},{1,9},{2,10},{3,11},{4,12},{5,13},{6,14},{7,15},{8,0},{9,1},... | collective-permute-start | bytes 122888 | tf_op jit(solution)/shard_map/ppermute | solution.py:50
  29.9 1.3 %collective-permute-start.8 = (bf16[16,2048]{1,0:T(8,128)(2,1)S(1)}, bf16[16,2048]{1,0:T(8,128)(2,1)S(1)}, u32[]{:S(2)}, u32[]{:S(2)}) collective-permute-start(bf16[16,2048]{1,0:T(8,128)(2,1)S(1)} %get-tuple-element.46), channel_id=1, source_target_pairs={{0,1},{1,0},{2,3},{3,2},{4,5},{5,4},{6,7},{7,6},{8,9},{9,8},{10,11... | collective-permute-start | bytes 196616 | tf_op jit(solution)/shard_map/ppermute | solution.py:50
  31.2 4.3 %collective-permute-start.9 = (bf16[16,2048]{1,0:T(8,128)(2,1)S(1)}, bf16[16,2048]{1,0:T(8,128)(2,1)S(1)}, u32[]{:S(2)}, u32[]{:S(2)}) collective-permute-start(bf16[16,2048]{1,0:T(8,128)(2,1)S(1)} %fusion.5.refs_0_), channel_id=1, source_target_pairs={{0,2},{1,3},{2,0},{3,1},{4,6},{5,7},{6,4},{7,5},{8,10},{9,11},{10,... | collective-permute-start | bytes 196616 | tf_op jit(solution)/shard_map/ppermute | solution.py:50
  32.9 2.7 %copy-start.2 = (bf16[16,2048]{1,0:T(8,128)(2,1)S(1)}, bf16[16,2048]{1,0:T(8,128)(2,1)}, u32[]{:S(2)}) copy-start(bf16[16,2048]{1,0:T(8,128)(2,1)} %hidden_hbm.1) | copy-start | bytes 196612
  35.7 5.7 %collective-permute-start.10 = (bf16[32,1024]{1,0:T(8,128)(2,1)S(1)}, bf16[32,1024]{1,0:T(8,128)(2,1)S(1)}, u32[]{:S(2)}, u32[]{:S(2)}) collective-permute-start(bf16[32,1024]{1,0:T(8,128)(2,1)S(1)} %pad_maximum_fusion.4), channel_id=1, source_target_pairs={{0,16},{1,25},{2,18},{3,27},{4,20},{5,29},{6,22},{7,31},{8,24},{9,... | collective-permute-start | bytes 196616 | tf_op jit(solution)/shard_map/ppermute | solution.py:67
  37.3 4.0 %collective-permute-start.11 = (bf16[16,1024]{1,0:T(8,128)(2,1)S(1)}, bf16[16,1024]{1,0:T(8,128)(2,1)S(1)}, u32[]{:S(2)}, u32[]{:S(2)}) collective-permute-start(bf16[16,1024]{1,0:T(8,128)(2,1)S(1)} %get-tuple-element.76), channel_id=1, source_target_pairs={{0,8},{1,9},{2,10},{3,11},{4,12},{5,13},{6,14},{7,15},{8,0},{9,1},... | collective-permute-start | bytes 98312 | tf_op jit(solution)/shard_map/ppermute | solution.py:50
  38.6 4.3 %copy-start.1 = (f32[2048]{0:T(1024)S(1)}, f32[2048]{0:T(1024)}, u32[]{:S(2)}) copy-start(f32[2048]{0:T(1024)} %param.28) | copy-start | bytes 24580
  41.4 5.3 %collective-permute-start.12 = (bf16[64,1024]{1,0:T(8,128)(2,1)S(1)}, bf16[64,1024]{1,0:T(8,128)(2,1)S(1)}, u32[]{:S(2)}, u32[]{:S(2)}) collective-permute-start(bf16[64,1024]{1,0:T(8,128)(2,1)S(1)} %pad_maximum_fusion.2.refs_0_), channel_id=1, source_target_pairs={{0,4},{1,5},{2,6},{3,7},{4,0},{5,1},{6,2},{7,3},{8,12},{9,13},{10,... | collective-permute-start | bytes 393224 | tf_op jit(solution)/shard_map/ppermute | solution.py:50
  42.9 3.9 %collective-permute-start.13 = (bf16[64,1024]{1,0:T(8,128)(2,1)S(1)}, bf16[64,1024]{1,0:T(8,128)(2,1)S(1)}, u32[]{:S(2)}, u32[]{:S(2)}) collective-permute-start(bf16[64,1024]{1,0:T(8,128)(2,1)S(1)} %pad_maximum_fusion.2.refs_0_), channel_id=1, source_target_pairs={{0,1},{1,0},{2,3},{3,2},{4,5},{5,4},{6,7},{7,6},{8,9},{9,8},{10,11... | collective-permute-start | bytes 393224 | tf_op jit(solution)/shard_map/ppermute | solution.py:50
  46.6 1.3 %collective-permute-start.14 = (bf16[64,1024]{1,0:T(8,128)(2,1)S(1)}, bf16[64,1024]{1,0:T(8,128)(2,1)S(1)}, u32[]{:S(2)}, u32[]{:S(2)}) collective-permute-start(bf16[64,1024]{1,0:T(8,128)(2,1)S(1)} %collective-permute-done.12.refs_1_), channel_id=1, source_target_pairs={{0,1},{1,0},{2,3},{3,2},{4,5},{5,4},{6,7},{7,6},{8,9},{9,8},{10,11... | collective-permute-start | bytes 393224 | tf_op jit(solution)/shard_map/ppermute | solution.py:50
  50.6 1.6 %collective-permute-start.15 = (bf16[2,128,512]{2,1,0:T(8,128)(2,1)S(1)}, bf16[2,128,512]{2,1,0:T(8,128)(2,1)S(1)}, u32[]{:S(2)}, u32[]{:S(2)}) collective-permute-start(bf16[2,128,512]{2,1,0:T(8,128)(2,1)S(1)} %get-tuple-element.58), channel_id=1, source_target_pairs={{0,1},{1,0},{2,3},{3,2},{4,5},{5,4},{6,7},{7,6},{8,9},{9,8},{10,11... | collective-permute-start | bytes 786440 | tf_op jit(solution)/shard_map/ppermute | solution.py:50
  52.3 4.3 %collective-permute-start.16 = (bf16[64,512]{1,0:T(8,128)(2,1)S(1)}, bf16[64,512]{1,0:T(8,128)(2,1)S(1)}, u32[]{:S(2)}, u32[]{:S(2)}) collective-permute-start(bf16[64,512]{1,0:T(8,128)(2,1)S(1)} %get-tuple-element.63), channel_id=1, source_target_pairs={{0,4},{1,5},{2,6},{3,7},{4,0},{5,1},{6,2},{7,3},{8,12},{9,13},{10,... | collective-permute-start | bytes 196616 | tf_op jit(solution)/shard_map/ppermute | solution.py:50
  53.9 5.6 %collective-permute-start.18 = (bf16[64,512]{1,0:T(8,128)(2,1)S(1)}, bf16[64,512]{1,0:T(8,128)(2,1)S(1)}, u32[]{:S(2)}, u32[]{:S(2)}) collective-permute-start(bf16[64,512]{1,0:T(8,128)(2,1)S(1)} %get-tuple-element.64), channel_id=1, source_target_pairs={{0,6},{1,7},{2,4},{3,5},{4,2},{5,3},{6,0},{7,1},{8,14},{9,15},{10,... | collective-permute-start | bytes 196616 | tf_op jit(solution)/shard_map/ppermute | solution.py:50
  55.1 4.5 %collective-permute-start.17 = (bf16[64,512]{1,0:T(8,128)(2,1)S(1)}, bf16[64,512]{1,0:T(8,128)(2,1)S(1)}, u32[]{:S(2)}, u32[]{:S(2)}) collective-permute-start(bf16[64,512]{1,0:T(8,128)(2,1)S(1)} %get-tuple-element.65), channel_id=1, source_target_pairs={{0,2},{1,3},{2,0},{3,1},{4,6},{5,7},{6,4},{7,5},{8,10},{9,11},{10,... | collective-permute-start | bytes 196616 | tf_op jit(solution)/shard_map/ppermute | solution.py:50
  59.6 5.6 %collective-permute-start.19 = (bf16[16,512]{1,0:T(8,128)(2,1)S(1)}, bf16[16,512]{1,0:T(8,128)(2,1)S(1)}, u32[]{:S(2)}, u32[]{:S(2)}) collective-permute-start(bf16[16,512]{1,0:T(8,128)(2,1)S(1)} %get-tuple-element.72), channel_id=1, source_target_pairs={{0,24},{1,25},{2,26},{3,27},{4,28},{5,29},{6,30},{7,31},{8,16},{9,... | collective-permute-start | bytes 49160 | tf_op jit(solution)/shard_map/ppermute | solution.py:50
  62.3 3.7 %collective-permute-start.21 = (bf16[16,512]{1,0:T(8,128)(2,1)S(1)}, bf16[16,512]{1,0:T(8,128)(2,1)S(1)}, u32[]{:S(2)}, u32[]{:S(2)}) collective-permute-start(bf16[16,512]{1,0:T(8,128)(2,1)S(1)} %get-tuple-element.73), channel_id=1, source_target_pairs={{0,8},{1,9},{2,10},{3,11},{4,12},{5,13},{6,14},{7,15},{8,0},{9,1},... | collective-permute-start | bytes 49160 | tf_op jit(solution)/shard_map/ppermute | solution.py:50
  62.3 4.6 %collective-permute-start.20 = (bf16[16,512]{1,0:T(8,128)(2,1)S(1)}, bf16[16,512]{1,0:T(8,128)(2,1)S(1)}, u32[]{:S(2)}, u32[]{:S(2)}) collective-permute-start(bf16[16,512]{1,0:T(8,128)(2,1)S(1)} %get-tuple-element.74), channel_id=1, source_target_pairs={{0,16},{1,17},{2,18},{3,19},{4,20},{5,21},{6,22},{7,23},{8,24},{9,... | collective-permute-start | bytes 49160 | tf_op jit(solution)/shard_map/ppermute | solution.py:50
